TPU v7x, 32 devices: a whole 2x2x4 slice. The times are simulated.
32 devices in a mesh: samp: 16 (over z, y, core), blk: 2 (over x).
Axes of the slice: x: 2, y: 2, z: 4, core: 2. Of those that a mesh axis runs over, the one named last changes fastest.
Arguments:
- genotypes: int32 [65536, 2048], P('samp', 'blk'), may hold values from 0 to 2
- traits: bfloat16 [65536, 64], P('samp'), may hold values from -6 to 6
- penalty_index: int32 [5], replicated, may hold values from 0 to 9
Outputs:
- level_gram: float32 [64, 10, 10], P('blk')
- level_cross: float32 [64, 10], P('blk')
All inputs are finite; a program needn't handle non-finite values.
Results may differ from a plain program's by a relative error of at most 0.0004.
Values may be sent and summed in bfloat16 or wider, within the bound.
No kernel may reach another device: no remote copies, remote signals or barrier semaphores. Data moves between devices by JAX's collectives and lax.ppermute only.
A program may use at most 192 MiB of HBM per device.

v0:
```python
import functools

import jax
import jax.numpy as jnp
from jax import lax
from jax.experimental import pallas as pl
from jax.experimental.pallas import tpu as pltpu
from jax.sharding import PartitionSpec as P

BLK = 128
SUB = 8
GROUP = 8
HI = lax.Precision.HIGHEST
NT = (((1,), (1,)), ((), ()))
TN = (((0,), (0,)), ((), ()))


def dot_hi(a, b):
    return jnp.dot(a, b, precision=HI, preferred_element_type=jnp.float32)


def dot_nt(a, b):
    return lax.dot_general(a, b, NT, precision=HI, preferred_element_type=jnp.float32)


def panel_rows(nvars):
    starts = [0]
    for j in range(nvars // BLK):
        starts.append(starts[-1] + nvars - BLK * j)
    return starts[:-1], starts[-1]


def side_rows(ntraits):
    return ntraits + SUB


def down(row):
    return jnp.transpose(jnp.broadcast_to(row, (BLK, BLK)))


def inverse_of(x):
    near = pl.reciprocal(x, approx=True)
    return near * (2.0 - x * near)


def split(x):
    first = x.astype(jnp.bfloat16)
    rest = x - first.astype(jnp.float32)
    second = rest.astype(jnp.bfloat16)
    return first, second, (rest - second.astype(jnp.float32)).astype(jnp.bfloat16)


def as_left(x):
    a, b, c = split(x)
    return jnp.concatenate([a, a, b, a, b, c], axis=1)


def as_right(x, axis):
    a, b, c = split(x)
    return jnp.concatenate([a, b, a, c, b, a], axis=axis)


def invert_tile(tile):
    strips = [tile[SUB * i:SUB * (i + 1), :] for i in range(BLK // SUB)]
    lane = lax.broadcasted_iota(jnp.int32, (SUB, BLK), 1)
    sub = lax.broadcasted_iota(jnp.int32, (SUB, BLK), 0)
    rows_at = [sub == j for j in range(SUB)]
    for k in range(BLK // SUB):
        at = SUB * k
        inside = (lane >= at) & (lane < at + SUB)
        eye = (lane - at == sub).astype(jnp.float32)
        cols = [jnp.broadcast_to(strips[k][:, at + j:at + j + 1], (SUB, BLK)) for j in range(SUB)]
        right = jnp.where(inside, eye, strips[k])
        for j in range(SUB):
            pivot = inverse_of(jnp.broadcast_to(cols[j][j:j + 1, :], (SUB, BLK)))
            step = jnp.where(rows_at[j], -1.0, cols[j])

            def move(x):
                return jnp.where(rows_at[j], 0.0, x) - (step * jnp.broadcast_to(x[j:j + 1, :], (SUB, BLK))) * pivot

            cols = cols[:j + 1] + [move(c) for c in cols[j + 1:]]
            right = move(right)
        tops = [jnp.broadcast_to(right[j:j + 1, :], (SUB, BLK)) for j in range(SUB)]
        fresh = []
        for i in range(BLK // SUB):
            if i == k:
                fresh.append(right)
                continue
            rest = jnp.where(inside, 0.0, strips[i])
            for j in range(SUB):
                rest = rest - jnp.broadcast_to(strips[i][:, at + j:at + j + 1], (SUB, BLK)) * tops[j]
            fresh.append(rest)
        strips = fresh
    return jnp.concatenate(strips, axis=0)


def piece_starts(rows):
    return [0, rows * 17 // 32, rows]


def gram_kernel(ntraits, rank_ref, geno_ref, traits_ref, near_ref, away_ref, kept_ref, *refs):
    nvars = geno_ref.shape[1]
    step = pl.program_id(0)
    half = pl.num_programs(0) // 2
    wide = 2 * BLK
    pieces, side, ysum, panels = refs[:2], refs[2], refs[3], refs[4:]

    @pl.when(step == 0)
    def _():
        side[...] = jnp.zeros_like(side)
        ysum[...] = jnp.zeros_like(ysum)
        for panel in panels:
            panel[...] = jnp.zeros_like(panel)

    dosage = geno_ref[...].astype(jnp.float32).astype(jnp.bfloat16)

    count = dosage.shape[0]
    for tile in range(piece_starts(geno_ref.shape[0] * 2)[-1] // count):
        @pl.when(step == tile)
        def _(tile=tile):
            starts = piece_starts(count * 2)
            for piece, first, end in zip(pieces, starts, starts[1:]):
                low, high = max(first, tile * count), min(end, (tile + 1) * count)
                if low < high:
                    piece[low - first:high - first, :] = dosage[low - tile * count:high - tile * count, :]

    @pl.when(step >= half)
    def _():
        kept_ref[...] = dosage

    for j, panel in enumerate(panels):
        left, right = dosage[:, wide * j:], dosage[:, wide * j:wide * (j + 1)]
        panel[...] += lax.dot_general(left, right, TN, preferred_element_type=jnp.float32)
    traits = traits_ref[...]
    rows = jnp.concatenate([traits, jnp.ones((2 * SUB, count), jnp.bfloat16)], axis=0)
    sums = jnp.dot(rows, dosage, preferred_element_type=jnp.float32)
    side[...] += sums[0:side.shape[0], :]
    ysum[...] += jnp.sum(traits.astype(jnp.float32), axis=1, keepdims=True)

    def hand_out(even, odd):
        rows = even.shape[0]

        def store(row, value):
            while value.shape[0] > 0:
                place, at = divmod(row, rows)
                size = min(value.shape[0], rows - at)
                (odd if place else even)[at:at + size, :] = value[:size, :]
                row, value = row + size, value[size:, :]

        starts, low = panel_rows(nvars)
        for j, start in enumerate(starts):
            skip = BLK * (j % 2)
            store(start, panels[j // 2][skip:, skip:skip + BLK])
        tall = side_rows(ntraits)
        for j in range(nvars // BLK):
            store(low + tall * j, side[:, BLK * j:BLK * (j + 1)])
        used = low + tall * (nvars // BLK) + ntraits
        store(used - ntraits, ysum[...])
        if used < 2 * rows:
            store(used, jnp.zeros((2 * rows - used, BLK), jnp.float32))

    last = step == pl.num_programs(0) - 1

    @pl.when(last & (rank_ref[1] == 0))
    def _():
        hand_out(near_ref, away_ref)

    @pl.when(last & (rank_ref[1] == 1))
    def _():
        hand_out(away_ref, near_ref)


def gram(genotypes, traits, place, members):
    count, nvars = genotypes.shape
    ntraits = traits.shape[0]
    steps = 4
    tile = count // steps
    half = steps // 2
    low = panel_rows(nvars)[1]
    share = 2 * SUB * members
    total = -(-(low + side_rows(ntraits) * (nvars // BLK) + ntraits) // share) * share

    def source(i, place_ref):
        return (lax.rem(i + half * (1 - place_ref[0]), steps), 0)

    def traits_source(i, place_ref):
        return (0, lax.rem(i + half * (1 - place_ref[0]), steps))

    starts = piece_starts(count // 2)
    sizes = [end - first for first, end in zip(starts, starts[1:])]
    return pl.pallas_call(
        functools.partial(gram_kernel, ntraits),
        grid_spec=pltpu.PrefetchScalarGridSpec(
            num_scalar_prefetch=1,
            grid=(steps,),
            in_specs=[pl.BlockSpec((tile, nvars), source), pl.BlockSpec((ntraits, tile), traits_source)],
            out_specs=[
                pl.BlockSpec((total // 2, BLK), lambda i, rank_ref: (0, 0)),
                pl.BlockSpec((total // 2, BLK), lambda i, rank_ref: (0, 0)),
                pl.BlockSpec((tile, nvars), lambda i, rank_ref: (jnp.maximum(i - half, 0), 0)),
            ]
            + [pl.BlockSpec((size, nvars), lambda i, rank_ref: (0, 0)) for size in sizes],
            scratch_shapes=[pltpu.VMEM((side_rows(ntraits), nvars), jnp.float32), pltpu.VMEM((ntraits, BLK), jnp.float32)]
            + [pltpu.VMEM((nvars - 2 * BLK * j, 2 * BLK), jnp.float32) for j in range(nvars // (2 * BLK))],
        ),
        out_shape=[jax.ShapeDtypeStruct((total // 2, BLK), jnp.float32)] * 2
        + [jax.ShapeDtypeStruct((size, nvars), jnp.bfloat16) for size in [count // 2] + sizes],
        compiler_params=pltpu.CompilerParams(vmem_limit_bytes=48 * 1024 * 1024),
        name="gram_sums",
    )(place, genotypes, traits)


def solve_kernel(nsamp, ntraits, lam_ref, near_a, near_b, far_a, far_b, *refs):
    coef_ref, mean_ref, aug, wide = refs[-4:]
    nvars = coef_ref.shape[1]
    nblocks = nvars // BLK
    starts, low = panel_rows(nvars)
    tall = side_rows(ntraits)
    lam = lam_ref[0, 0]
    lower = lax.rem(lax.axis_index("samp"), 2) == 0
    quarter = near_a.shape[0]
    pairs = [(near_a, far_a), (near_b, far_b), (far_a, near_a), (far_b, near_b)]

    def read(row, count):
        found = []
        while count > 0:
            place, at = divmod(row, quarter)
            size = min(count, quarter - at)
            even, odd = pairs[place]
            found.append(jnp.where(lower, even[at:at + size, :], odd[at:at + size, :]))
            row, count = row + size, count - size
        return found[0] if len(found) == 1 else jnp.concatenate(found, axis=0)

    eye = lax.broadcasted_iota(jnp.int32, (BLK, BLK), 0) == lax.broadcasted_iota(jnp.int32, (BLK, BLK), 1)
    sides = [read(low + tall * j, tall) for j in range(nblocks)]
    means = [side[ntraits:ntraits + 1, :] / nsamp for side in sides]
    means_down = [down(mean) for mean in means]
    ysum = read(low + tall * nblocks, ntraits)
    for j in range(nblocks):
        span = slice(BLK * j, BLK * (j + 1))
        mean_ref[:, span] = jnp.broadcast_to(means[j], (SUB, BLK))
        for i in range(j, nblocks):
            value = read(starts[j] + BLK * (i - j), BLK) - nsamp * means_down[i] * means[j]
            if i == j:
                value = value + jnp.where(eye, lam * (value / nsamp + 1e-05), 0.0)
            aug[BLK * i:BLK * (i + 1), span] = value
        aug[nvars:nvars + ntraits, span] = sides[j][0:ntraits, :] - ysum * means[j]
    end = nvars + ntraits
    inverse = invert_tile(aug[0:BLK, 0:BLK])
    for k in range(nblocks):
        span = slice(BLK * k, BLK * (k + 1))
        first = BLK * (k + 1)
        panel = aug[first:end, span]
        mult = jnp.dot(as_left(panel), as_right(inverse, 0), preferred_element_type=jnp.float32)
        wide[first:end, span] = mult
        if k == nblocks - 1:
            break
        left, right = as_left(mult), as_right(panel, 1)
        j = k + 1
        while j < nblocks:
            top = BLK * j
            size = BLK if j == k + 1 or j == nblocks - 1 else 2 * BLK
            at = top - first
            aug[top:end, top:top + size] -= lax.dot_general(left[at:, :], right[at:at + size, :], NT, preferred_element_type=jnp.float32)
            if j == k + 1:
                inverse = invert_tile(aug[top:top + BLK, top:top + BLK])
            j += size // BLK
    solved = wide[nvars:end, nvars - BLK:nvars]
    coef_ref[:, nvars - BLK:nvars] = solved.astype(jnp.bfloat16)
    for k in range(nblocks - 2, -1, -1):
        span = slice(BLK * k, BLK * (k + 1))
        found = wide[nvars:end, span] - dot_hi(solved, wide[BLK * (k + 1):nvars, span])
        coef_ref[:, span] = found.astype(jnp.bfloat16)
        solved = jnp.concatenate([found, solved], axis=1)


def solve(pieces, lam, arrived, nsamp, nvars, ntraits):
    return pl.pallas_call(
        functools.partial(solve_kernel, nsamp, ntraits),
        out_shape=[jax.ShapeDtypeStruct((ntraits, nvars), jnp.bfloat16), jax.ShapeDtypeStruct((SUB, nvars), jnp.float32)],
        in_specs=[pl.BlockSpec(memory_space=pltpu.SMEM)]
        + [pl.BlockSpec(memory_space=pltpu.VMEM)] * 4
        + [pl.BlockSpec(memory_space=pl.ANY)] * len(arrived),
        out_specs=[pl.BlockSpec(memory_space=pltpu.VMEM)] * 2,
        scratch_shapes=[
            pltpu.VMEM((nvars + ntraits, nvars), jnp.float32),
            pltpu.VMEM((nvars + ntraits, nvars), jnp.float32),
        ],
        compiler_params=pltpu.CompilerParams(vmem_limit_bytes=48 * 1024 * 1024),
        cost_estimate=pl.CostEstimate(flops=46 * 10**9, bytes_accessed=10**6, transcendentals=0),
        name="ridge_solve",
    )(lam, *pieces, *arrived)


def level_kernel(npen, own_ref, coef_ref, mean_ref, far_mean_ref, traits_ref, *refs):
    rank = lax.axis_index("blk")
    ntraits = coef_ref.shape[2]
    nvars = own_ref.shape[1]
    count = own_ref.shape[0]
    stack = 2 * npen
    tile = 512
    pieces, (out_ref, pred, other_ref) = refs[:-3], refs[-3:]
    low = 0
    for piece in pieces:
        other_ref[low:low + piece.shape[0], :] = piece[...]
        low += piece.shape[0]
    for place in range(2):
        block = rank if place == 0 else 1 - rank
        source = own_ref if place == 0 else other_ref
        mean = (mean_ref if place == 0 else far_mean_ref)[0:1, :]
        coef = jnp.concatenate([coef_ref[r, block] for r in range(npen)], axis=0)
        offset = jnp.sum(coef.astype(jnp.float32) * mean, axis=1, keepdims=True)
        low = pl.multiple_of(block * (npen * ntraits), npen * ntraits)
        for n in range(0, count, tile):
            value = lax.dot_general(coef, source[n:n + tile, :], NT, preferred_element_type=jnp.float32)
            pred[pl.ds(low, npen * ntraits), n:n + tile] = value - offset
    pred[stack * ntraits:(stack + 1) * ntraits, :] = traits_ref[...].astype(jnp.float32)
    lane = lax.broadcasted_iota(jnp.int32, (SUB, BLK), 1)
    for t in range(0, ntraits, SUB):
        acc = jnp.zeros((SUB, BLK), jnp.float32)
        for i in range(stack):
            left = pred[i * ntraits + t:i * ntraits + t + SUB, :]
            for j in range(i, stack + 1):
                term = jnp.sum(left * pred[j * ntraits + t:j * ntraits + t + SUB, :], axis=1, keepdims=True)
                if j < stack:
                    acc = jnp.where((lane == i * stack + j) | (lane == j * stack + i), term, acc)
                else:
                    acc = jnp.where(lane == stack * stack + i, term, acc)
        out_ref[t:t + SUB, :] = acc


def level_sums(own, others, coefs, mean, far_mean, traits, npen):
    ntraits = traits.shape[0]
    count = own.shape[0]
    vmem = pl.BlockSpec(memory_space=pltpu.VMEM)
    return pl.pallas_call(
        functools.partial(level_kernel, npen),
        out_shape=jax.ShapeDtypeStruct((ntraits, BLK), jnp.float32),
        in_specs=[vmem] * (5 + len(others)),
        out_specs=pl.BlockSpec(memory_space=pltpu.VMEM),
        scratch_shapes=[
            pltpu.VMEM(((2 * npen + 1) * ntraits, count), jnp.float32),
            pltpu.VMEM(own.shape, own.dtype),
        ],
        compiler_params=pltpu.CompilerParams(vmem_limit_bytes=56 * 1024 * 1024),
        name="level_sums",
    )(own, coefs, mean, far_mean, traits, *others)


def swapped(x, bit):
    return lax.ppermute(x, "samp", [(i, i ^ (1 << bit)) for i in range(lax.axis_size("samp"))])


def place_bit(bit):
    return lax.rem(lax.div(lax.axis_index("samp"), 1 << bit), 2)


def stack_kernel(near_ref, far_ref, piece_ref, out_ref):
    rank = lax.axis_index("blk")
    out_ref[rank] = near_ref[...]
    out_ref[1 - rank] = far_ref[...]


def stacked(near, far, piece):
    return pl.pallas_call(
        stack_kernel,
        out_shape=jax.ShapeDtypeStruct((2,) + near.shape, near.dtype),
        in_specs=[pl.BlockSpec(memory_space=pltpu.VMEM)] * 2 + [pl.BlockSpec(memory_space=pl.ANY)],
        out_specs=pl.BlockSpec(memory_space=pltpu.VMEM),
        cost_estimate=pl.CostEstimate(flops=10**6, bytes_accessed=10**5, transcendentals=0),
        name="stack_blocks",
    )(near, far, piece)


def halved(x, bit):
    rows = x.shape[0] // 2
    mine = place_bit(bit)
    far = swapped(lax.dynamic_slice_in_dim(x, (1 - mine) * rows, rows, 0), bit)
    return lax.dynamic_slice_in_dim(x, mine * rows, rows, 0) + far


def doubled(x, bit):
    far = swapped(x, bit)
    even = place_bit(bit) == 0
    return jnp.concatenate([jnp.where(even, x, far), jnp.where(even, far, x)], axis=0)


def all_sums(x, away):
    bits = list(range(1, lax.axis_size("samp").bit_length() - 1))
    x = x + swapped(away, 0)
    rows = x.shape[0] // 2
    near = []
    for part, order in ((x[:rows], bits), (x[rows:], bits[1:] + bits[:1])):
        for bit in order:
            part = halved(part, bit)
        for bit in reversed(order):
            part = doubled(part, bit)
        near.append(part)
    return near + [swapped(part, 0) for part in near]


def small_sum(x):
    for bit in range(lax.axis_size("samp").bit_length() - 1):
        x = x + swapped(x, bit)
    return x


def level_from_predictions(coefs, mean, dosage, traits, nvars):
    coef = coefs.transpose(0, 2, 1)
    ntraits = traits.shape[1]
    offset = jnp.einsum("rmt,m->rt", coef.astype(jnp.float32), mean, precision=HI)
    pred = jnp.einsum("rmt,nm->trn", coef, dosage, preferred_element_type=jnp.float32)
    pred = (pred - offset.T[:, :, None]).astype(jnp.bfloat16)
    local_traits = ntraits // lax.axis_size("blk")
    parts = lax.all_to_all(pred[None], "blk", split_axis=1, concat_axis=0, tiled=True)
    mine = lax.dynamic_slice_in_dim(traits, lax.axis_index("blk") * local_traits, local_traits, 1)
    gram = jnp.einsum("btrn,ctsn->tbrcs", parts, parts, preferred_element_type=jnp.float32)
    cross = jnp.einsum("btrn,nt->tbr", parts, mine, preferred_element_type=jnp.float32)
    count, stack = parts.shape[1], parts.shape[0] * parts.shape[2]
    gram, cross = lax.psum((gram.reshape(count, stack, stack), cross.reshape(count, stack)), "samp")
    return gram / nvars, cross / nvars


def local(genotypes, traits, penalty_index):
    count, nvars = genotypes.shape
    ntraits = traits.shape[1]
    npen = penalty_index.shape[0]
    nblk = lax.axis_size("blk")
    members = lax.axis_size("samp")
    nsamp = float(count * members)
    samp_rank = lax.axis_index("samp")
    blk_rank = lax.axis_index("blk")
    paired = nblk == 2
    place = jnp.stack([blk_rank if paired else jnp.int32(0), place_bit(0)])
    turned = traits.T
    near, away, kept, *sent = gram(genotypes, turned, place, members)
    others = [lax.ppermute(piece, "blk", [(0, 1), (1, 0)]) for piece in sent] if paired else []
    pieces = all_sums(near, away)
    lam = nsamp * jnp.exp2((penalty_index.astype(jnp.float32) - 8.0) / 2.0)
    mine = lax.dynamic_index_in_dim(lam, (samp_rank % GROUP) % npen, 0, keepdims=True).reshape(1, 1)
    coef, mean = solve(pieces, mine, others[:1], nsamp, nvars, ntraits)
    groups = [list(range(g, g + GROUP)) for g in range(0, members, GROUP)]
    if not paired:
        coefs = lax.all_gather(coef, "samp", axis_index_groups=groups)[:npen]
        dosage = genotypes.astype(jnp.bfloat16)
        return level_from_predictions(coefs, mean[0], dosage, traits, nvars)
    coef_far = lax.ppermute(coef, "blk", [(0, 1), (1, 0)])
    mean_far = lax.ppermute(mean, "blk", [(0, 1), (1, 0)])
    both = stacked(coef, coef_far, others[1])
    coefs = lax.all_gather(both, "samp", axis_index_groups=groups)
    rows = lax.dynamic_slice_in_dim(turned, blk_rank * (count // 2), count // 2, 1)
    found = level_sums(kept, others, coefs, mean, mean_far, rows, npen)
    stack = nblk * npen
    each = ntraits // nblk
    far = lax.ppermute(lax.dynamic_slice_in_dim(found, (1 - blk_rank) * each, each, 0), "blk", [(0, 1), (1, 0)])
    found = small_sum(lax.dynamic_slice_in_dim(found, blk_rank * each, each, 0) + far) / nvars
    return found[:, :stack * stack].reshape(each, stack, stack), found[:, stack * stack:stack * stack + stack]


def solution(mesh):
    placed = (P("samp", "blk"), P("samp", None), P())
    return jax.shard_map(
        local,
        mesh=mesh,
        in_specs=placed,
        out_specs=(P("blk", None, None), P("blk", None)),
        check_vma=False,
    )
```

profile of v0, /device:TPU:0, one launch (start us, length us, event | category | flops | bytes accessed | tf_op | source)
XLA Modules:
  0.0 200.4 jit_solution(15451643338699255096)
XLA Ops:
  7.3 1.0 copy-done.1
  8.3 16.6 %gram_sums.1 = (f32[2688,128]{1,0:T(8,128)S(1)}, f32[2688,128]{1,0:T(8,128)S(1)}, bf16[2048,1024]{1,0:T(8,128)(2,1)}, bf16[1088,1024]{1,0:T(8,128)(2,1)}, bf16[960,1024]{1,0:T(8,128)(2,1)}) custom-call(s32[2]{0:T(128)S(1)} %pad_add_fusion.rank_ref, s32[4096,1024]{1,0:T(8,128)} %geno_ref.1, bf16[64,4096]{1,0:T(8,128)(2,1)S(1)} %bitcast.10), custom_call_target="tpu_custom_call" | custom-call | tf_op jit(solution)/shard_map/gram_sums/pallas_call | solution.py:191
  25.4 2.9 %collective-permute-done = f32[2688,128]{1,0:T(8,128)} collective-permute-done((f32[2688,128]{1,0:T(8,128)S(1)}, f32[2688,128]{1,0:T(8,128)}, u32[]{:S(2)}, u32[]{:S(2)}) %collective-permute-start) | collective-permute-done | bytes 1376288 | tf_op jit(solution)/shard_map/ppermute | solution.py:351
  28.3 1.5 add.96
  29.9 0.8 constant_dynamic-slice_fusion.3
  30.7 3.0 %collective-permute-start.7 = (f32[672,128]{1,0:T(8,128)}, f32[672,128]{1,0:T(8,128)S(1)}, u32[]{:S(2)}, u32[]{:S(2)}) collective-permute-start(f32[672,128]{1,0:T(8,128)} %constant_dynamic-slice_fusion.3), channel_id=1, source_target_pairs={{0,8},{2,10},{4,12},{6,14},{8,0},{10,2},{12,4},{14,6},{16,24},{18,... | collective-permute-start | bytes 1032200 | tf_op jit(solution)/shard_map/ppermute | solution.py:351
  33.7 1.5 collective-permute-start.15
  35.2 1.6 collective-permute-start.1
  36.8 5.5 %collective-permute-done.7 = f32[672,128]{1,0:T(8,128)S(1)} collective-permute-done((f32[672,128]{1,0:T(8,128)}, f32[672,128]{1,0:T(8,128)S(1)}, u32[]{:S(2)}, u32[]{:S(2)}) %collective-permute-start.7) | collective-permute-done | bytes 344096 | tf_op jit(solution)/shard_map/ppermute | solution.py:351
  42.2 1.0 dynamic-slice_add_fusion
  43.3 2.8 %collective-permute-start.8 = (f32[336,128]{1,0:T(8,128)S(1)}, f32[336,128]{1,0:T(8,128)S(1)}, u32[]{:S(2)}, u32[]{:S(2)}) collective-permute-start(f32[336,128]{1,0:T(8,128)S(1)} %constant_dynamic-slice_fusion.2), channel_id=1, source_target_pairs={{0,16},{2,18},{4,20},{6,22},{8,24},{10,26},{12,28},{14,30},{16,0},... | collective-permute-start | bytes 516104 | tf_op jit(solution)/shard_map/ppermute | solution.py:351
  46.2 1.6 collective-permute-start.2
  47.8 6.1 %collective-permute-done.8 = f32[336,128]{1,0:T(8,128)S(1)} collective-permute-done((f32[336,128]{1,0:T(8,128)S(1)}, f32[336,128]{1,0:T(8,128)S(1)}, u32[]{:S(2)}, u32[]{:S(2)}) %collective-permute-start.8) | collective-permute-done | bytes 172064 | tf_op jit(solution)/shard_map/ppermute | solution.py:351
  54.0 1.4 collective-permute-start.9
  56.1 2.4 %collective-permute-done.9 = f32[168,128]{1,0:T(8,128)S(1)} collective-permute-done((f32[168,128]{1,0:T(8,128)S(1)}, f32[168,128]{1,0:T(8,128)S(1)}, u32[]{:S(2)}, u32[]{:S(2)}) %collective-permute-start.9) | collective-permute-done | bytes 86048 | tf_op jit(solution)/shard_map/ppermute | solution.py:351
  58.5 1.4 collective-permute-start.10
  60.0 2.9 %collective-permute-done.3 = f32[168,128]{1,0:T(8,128)S(1)} collective-permute-done((f32[168,128]{1,0:T(8,128)S(1)}, f32[168,128]{1,0:T(8,128)S(1)}, u32[]{:S(2)}, u32[]{:S(2)}) %collective-permute-start.3) | collective-permute-done | bytes 86048 | tf_op jit(solution)/shard_map/ppermute | solution.py:351
  63.1 2.9 %collective-permute-start.11 = (f32[336,128]{1,0:T(8,128)S(1)}, f32[336,128]{1,0:T(8,128)S(1)}, u32[]{:S(2)}, u32[]{:S(2)}) collective-permute-start(f32[336,128]{1,0:T(8,128)S(1)} %pad_maximum_fusion.5), channel_id=1, source_target_pairs={{0,16},{2,18},{4,20},{6,22},{8,24},{10,26},{12,28},{14,30},{16,0},... | collective-permute-start | bytes 516104 | tf_op jit(solution)/shard_map/ppermute | solution.py:351
  66.0 6.3 %collective-permute-done.4 = f32[168,128]{1,0:T(8,128)S(1)} collective-permute-done((f32[168,128]{1,0:T(8,128)S(1)}, f32[168,128]{1,0:T(8,128)S(1)}, u32[]{:S(2)}, u32[]{:S(2)}) %collective-permute-start.4) | collective-permute-done | bytes 86048 | tf_op jit(solution)/shard_map/ppermute | solution.py:351
  72.4 1.7 collective-permute-done.11
  74.6 5.2 %collective-permute-done.5 = f32[336,128]{1,0:T(8,128)S(1)} collective-permute-done((f32[336,128]{1,0:T(8,128)S(1)}, f32[336,128]{1,0:T(8,128)S(1)}, u32[]{:S(2)}, u32[]{:S(2)}) %collective-permute-start.5) | collective-permute-done | bytes 172064 | tf_op jit(solution)/shard_map/ppermute | solution.py:351
  79.9 3.8 %collective-permute-done.12 = f32[672,128]{1,0:T(8,128)S(1)} collective-permute-done((f32[672,128]{1,0:T(8,128)S(1)}, f32[672,128]{1,0:T(8,128)S(1)}, u32[]{:S(2)}, u32[]{:S(2)}) %collective-permute-start.12) | collective-permute-done | bytes 344096 | tf_op jit(solution)/shard_map/ppermute | solution.py:351
  83.9 3.2 %collective-permute-done.6 = f32[672,128]{1,0:T(8,128)S(1)} collective-permute-done((f32[672,128]{1,0:T(8,128)S(1)}, f32[672,128]{1,0:T(8,128)S(1)}, u32[]{:S(2)}, u32[]{:S(2)}) %collective-permute-start.6) | collective-permute-done | bytes 344096 | tf_op jit(solution)/shard_map/ppermute | solution.py:351
  87.1 0.9 pad_maximum_fusion.near_a
  88.0 1.5 collective-permute-start.17
  90.5 43.8 %ridge_solve.1 = (bf16[64,1024]{1,0:T(8,128)(2,1)S(1)}, f32[8,1024]{1,0:T(8,128)S(1)}) custom-call(f32[1,1]{1,0:T(1,128)} %bitcast.3.lam_ref, f32[1344,128]{1,0:T(8,128)} %pad_maximum_fusion.near_a, f32[1344,128]{1,0:T(8,128)S(1)} %pad_maximum_fusion.1.near_b, f32[1344,128]{1,0:T(8,128)} %collective-permute-done.13.far_a, ...), custom_call_target="tpu_custom_call" | custom-call | flops 46000001024 | bytes 1000000 | tf_op jit(solution)/shard_map/ridge_solve/pallas_call | solution.py:278
  134.4 1.5 collective-permute-start.16
  135.9 4.1 %collective-permute-done.16.far_ref = bf16[64,1024]{1,0:T(8,128)(2,1)S(1)} collective-permute-done((bf16[64,1024]{1,0:T(8,128)(2,1)S(1)}, bf16[64,1024]{1,0:T(8,128)(2,1)S(1)}, u32[]{:S(2)}, u32[]{:S(2)}) %collective-permute-start.16) | collective-permute-done | bytes 131104 | tf_op jit(solution)/shard_map/ppermute | solution.py:447
  140.0 0.6 copy-done.6
  140.6 1.7 stack_blocks.1
  142.4 1.5 collective-permute-start.18
  143.9 0.7 dynamic-slice_bitcast_fusion.traits_ref
  144.6 1.7 collective-permute-done.18.far_mean_ref
  146.4 17.0 %all-gather.3.cloned.1.call-done = bf16[16,64,1024]{2,1,0:T(8,128)(2,1)} async-done(((bf16[2,64,1024]{2,1,0:T(8,128)(2,1)}), bf16[16,64,1024]{2,1,0:T(8,128)(2,1)}) %all-gather.3.cloned.1.call-update) | async-done | bytes 2097168 | tf_op jit(solution)/shard_map/all_gather | solution.py:450
  163.4 10.0 %level_sums.1 = f32[64,128]{1,0:T(8,128)} custom-call(bf16[2048,1024]{1,0:T(8,128)(2,1)} %get-tuple-element.9.own_ref, bf16[8,2,64,1024]{3,2,1,0:T(8,128)(2,1)} %bitcast.11, f32[8,1024]{1,0:T(8,128)} %copy-done.4, f32[8,1024]{1,0:T(8,128)} %copy-done.7, bf16[64,2048]{1,0:T(8,128)(2,1)} %dynamic-slice_bitcast_fusion.traits_ref, bf16[1088,1024]{1,0:T(8,128)(2,1)} %copy-done, ...), custom_call_target="tpu_custom_call" | custom-call | tf_op jit(solution)/shard_map/level_sums/pallas_call | solution.py:336
  173.4 0.7 constant_dynamic-slice_fusion
  174.1 1.6 collective-permute-start.19
  175.7 2.1 %collective-permute-done.19 = f32[32,128]{1,0:T(8,128)S(1)} collective-permute-done((f32[32,128]{1,0:T(8,128)S(1)}, f32[32,128]{1,0:T(8,128)S(1)}, u32[]{:S(2)}, u32[]{:S(2)}) %collective-permute-start.19) | collective-permute-done | bytes 16416 | tf_op jit(solution)/shard_map/ppermute | solution.py:455
  177.8 0.7 dynamic-slice_add_fusion.6
  178.6 1.2 collective-permute-done.20
  179.7 1.5 collective-permute-start.21
  181.2 2.2 %collective-permute-done.21 = f32[32,128]{1,0:T(8,128)S(1)} collective-permute-done((f32[32,128]{1,0:T(8,128)S(1)}, f32[32,128]{1,0:T(8,128)S(1)}, u32[]{:S(2)}, u32[]{:S(2)}) %collective-permute-start.21) | collective-permute-done | bytes 16416 | tf_op jit(solution)/shard_map/ppermute | solution.py:351
  183.5 1.6 collective-permute-start.22
  185.1 2.2 %collective-permute-done.22 = f32[32,128]{1,0:T(8,128)S(1)} collective-permute-done((f32[32,128]{1,0:T(8,128)S(1)}, f32[32,128]{1,0:T(8,128)S(1)}, u32[]{:S(2)}, u32[]{:S(2)}) %collective-permute-start.22) | collective-permute-done | bytes 16416 | tf_op jit(solution)/shard_map/ppermute | solution.py:351
  187.2 2.6 %collective-permute-start.23 = (f32[32,128]{1,0:T(8,128)S(1)}, f32[32,128]{1,0:T(8,128)S(1)}, u32[]{:S(2)}, u32[]{:S(2)}) collective-permute-start(f32[32,128]{1,0:T(8,128)S(1)} %add.121), channel_id=1, source_target_pairs={{0,16},{2,18},{4,20},{6,22},{8,24},{10,26},{12,28},{14,30},{16,0},... | collective-permute-start | bytes 49160 | tf_op jit(solution)/shard_map/ppermute | solution.py:351
  189.8 2.1 %collective-permute-done.23 = f32[32,128]{1,0:T(8,128)S(1)} collective-permute-done((f32[32,128]{1,0:T(8,128)S(1)}, f32[32,128]{1,0:T(8,128)S(1)}, u32[]{:S(2)}, u32[]{:S(2)}) %collective-permute-start.23) | collective-permute-done | bytes 16416 | tf_op jit(solution)/shard_map/ppermute | solution.py:351
  192.0 0.6 reshape.11
  192.7 0.7 copy.10
  (65 shorter events, 3.9 us)
Async XLA Ops:
  7.2 156.2 %all-gather.3.cloned.1.call-start = ((), (), s32[]{:S(2)}) async-start(), calls=%async_computation | async-start | bytes 2359296 | tf_op jit(solution)/shard_map/all_gather | solution.py:450
  7.3 1.0 copy-start.1
  24.9 3.4 %collective-permute-start = (f32[2688,128]{1,0:T(8,128)S(1)}, f32[2688,128]{1,0:T(8,128)}, u32[]{:S(2)}, u32[]{:S(2)}) collective-permute-start(f32[2688,128]{1,0:T(8,128)S(1)} %get-tuple-element.11), channel_id=1, source_target_pairs={{0,2},{2,0},{4,6},{6,4},{8,10},{10,8},{12,14},{14,12},{16,18},{18,... | collective-permute-start | bytes 4128776 | tf_op jit(solution)/shard_map/ppermute | solution.py:351
  29.9 3.8 %copy-start.5 = (f32[1344,128]{1,0:T(8,128)}, f32[1344,128]{1,0:T(8,128)S(1)}, u32[]{:S(2)}) copy-start(f32[1344,128]{1,0:T(8,128)S(1)} %get-tuple-element.22) | copy-start | bytes 2064388
  30.7 11.5 %collective-permute-start.7 = (f32[672,128]{1,0:T(8,128)}, f32[672,128]{1,0:T(8,128)S(1)}, u32[]{:S(2)}, u32[]{:S(2)}) collective-permute-start(f32[672,128]{1,0:T(8,128)} %constant_dynamic-slice_fusion.3), channel_id=1, source_target_pairs={{0,8},{2,10},{4,12},{6,14},{8,0},{10,2},{12,4},{14,6},{16,24},{18,... | collective-permute-start | bytes 1032200 | tf_op jit(solution)/shard_map/ppermute | solution.py:351
  33.7 56.5 %collective-permute-start.15 = (bf16[1088,1024]{1,0:T(8,128)(2,1)}, bf16[1088,1024]{1,0:T(8,128)(2,1)S(1)}, u32[]{:S(2)}, u32[]{:S(2)}) collective-permute-start(bf16[1088,1024]{1,0:T(8,128)(2,1)} %get-tuple-element.12), channel_id=1, source_target_pairs={{0,1},{1,0},{2,3},{3,2},{4,5},{5,4},{6,7},{7,6},{8,9},{9,8},{10,11... | collective-permute-start | bytes 6684680 | tf_op jit(solution)/shard_map/ppermute | solution.py:437
  35.2 10.9 %collective-permute-start.1 = (f32[672,128]{1,0:T(8,128)S(1)}, f32[672,128]{1,0:T(8,128)S(1)}, u32[]{:S(2)}, u32[]{:S(2)}) collective-permute-start(f32[672,128]{1,0:T(8,128)S(1)} %constant_dynamic-slice_fusion.6), channel_id=1, source_target_pairs={{0,4},{2,6},{4,0},{6,2},{8,12},{10,14},{12,8},{14,10},{16,20},{18,... | collective-permute-start | bytes 1032200 | tf_op jit(solution)/shard_map/ppermute | solution.py:351
  43.3 10.7 %collective-permute-start.8 = (f32[336,128]{1,0:T(8,128)S(1)}, f32[336,128]{1,0:T(8,128)S(1)}, u32[]{:S(2)}, u32[]{:S(2)}) collective-permute-start(f32[336,128]{1,0:T(8,128)S(1)} %constant_dynamic-slice_fusion.2), channel_id=1, source_target_pairs={{0,16},{2,18},{4,20},{6,22},{8,24},{10,26},{12,28},{14,30},{16,0},... | collective-permute-start | bytes 516104 | tf_op jit(solution)/shard_map/ppermute | solution.py:351
  46.2 9.2 %collective-permute-start.2 = (f32[336,128]{1,0:T(8,128)S(1)}, f32[336,128]{1,0:T(8,128)S(1)}, u32[]{:S(2)}, u32[]{:S(2)}) collective-permute-start(f32[336,128]{1,0:T(8,128)S(1)} %constant_dynamic-slice_fusion.5), channel_id=1, source_target_pairs={{0,8},{2,10},{4,12},{6,14},{8,0},{10,2},{12,4},{14,6},{16,24},{18,... | collective-permute-start | bytes 516104 | tf_op jit(solution)/shard_map/ppermute | solution.py:351
  54.0 4.6 %collective-permute-start.9 = (f32[168,128]{1,0:T(8,128)S(1)}, f32[168,128]{1,0:T(8,128)S(1)}, u32[]{:S(2)}, u32[]{:S(2)}) collective-permute-start(f32[168,128]{1,0:T(8,128)S(1)} %constant_dynamic-slice_fusion.1), channel_id=1, source_target_pairs={{0,4},{2,6},{4,0},{6,2},{8,12},{10,14},{12,8},{14,10},{16,20},{18,... | collective-permute-start | bytes 258056 | tf_op jit(solution)/shard_map/ppermute | solution.py:351
  55.5 7.4 %collective-permute-start.3 = (f32[168,128]{1,0:T(8,128)S(1)}, f32[168,128]{1,0:T(8,128)S(1)}, u32[]{:S(2)}, u32[]{:S(2)}) collective-permute-start(f32[168,128]{1,0:T(8,128)S(1)} %constant_dynamic-slice_fusion.4), channel_id=1, source_target_pairs={{0,16},{2,18},{4,20},{6,22},{8,24},{10,26},{12,28},{14,30},{16,0},... | collective-permute-start | bytes 258056 | tf_op jit(solution)/shard_map/ppermute | solution.py:351
  58.5 4.6 %collective-permute-start.10 = (f32[168,128]{1,0:T(8,128)S(1)}, f32[168,128]{1,0:T(8,128)S(1)}, u32[]{:S(2)}, u32[]{:S(2)}) collective-permute-start(f32[168,128]{1,0:T(8,128)S(1)} %dynamic-slice_add_fusion.4), channel_id=1, source_target_pairs={{0,4},{2,6},{4,0},{6,2},{8,12},{10,14},{12,8},{14,10},{16,20},{18,... | collective-permute-start | bytes 258056 | tf_op jit(solution)/shard_map/ppermute | solution.py:351
  62.9 9.4 %collective-permute-start.4 = (f32[168,128]{1,0:T(8,128)S(1)}, f32[168,128]{1,0:T(8,128)S(1)}, u32[]{:S(2)}, u32[]{:S(2)}) collective-permute-start(f32[168,128]{1,0:T(8,128)S(1)} %dynamic-slice_add_fusion.5), channel_id=1, source_target_pairs={{0,16},{2,18},{4,20},{6,22},{8,24},{10,26},{12,28},{14,30},{16,0},... | collective-permute-start | bytes 258056 | tf_op jit(solution)/shard_map/ppermute | solution.py:351
  63.1 11.0 %collective-permute-start.11 = (f32[336,128]{1,0:T(8,128)S(1)}, f32[336,128]{1,0:T(8,128)S(1)}, u32[]{:S(2)}, u32[]{:S(2)}) collective-permute-start(f32[336,128]{1,0:T(8,128)S(1)} %pad_maximum_fusion.5), channel_id=1, source_target_pairs={{0,16},{2,18},{4,20},{6,22},{8,24},{10,26},{12,28},{14,30},{16,0},... | collective-permute-start | bytes 516104 | tf_op jit(solution)/shard_map/ppermute | solution.py:351
  72.3 7.4 %collective-permute-start.5 = (f32[336,128]{1,0:T(8,128)S(1)}, f32[336,128]{1,0:T(8,128)S(1)}, u32[]{:S(2)}, u32[]{:S(2)}) collective-permute-start(f32[336,128]{1,0:T(8,128)S(1)} %pad_maximum_fusion.4), channel_id=1, source_target_pairs={{0,8},{2,10},{4,12},{6,14},{8,0},{10,2},{12,4},{14,6},{16,24},{18,... | collective-permute-start | bytes 516104 | tf_op jit(solution)/shard_map/ppermute | solution.py:351
  74.2 9.5 %collective-permute-start.12 = (f32[672,128]{1,0:T(8,128)S(1)}, f32[672,128]{1,0:T(8,128)S(1)}, u32[]{:S(2)}, u32[]{:S(2)}) collective-permute-start(f32[672,128]{1,0:T(8,128)S(1)} %pad_maximum_fusion.3), channel_id=1, source_target_pairs={{0,8},{2,10},{4,12},{6,14},{8,0},{10,2},{12,4},{14,6},{16,24},{18,... | collective-permute-start | bytes 1032200 | tf_op jit(solution)/shard_map/ppermute | solution.py:351
  79.8 7.3 %collective-permute-start.6 = (f32[672,128]{1,0:T(8,128)S(1)}, f32[672,128]{1,0:T(8,128)S(1)}, u32[]{:S(2)}, u32[]{:S(2)}) collective-permute-start(f32[672,128]{1,0:T(8,128)S(1)} %pad_maximum_fusion.2), channel_id=1, source_target_pairs={{0,4},{2,6},{4,0},{6,2},{8,12},{10,14},{12,8},{14,10},{16,20},{18,... | collective-permute-start | bytes 1032200 | tf_op jit(solution)/shard_map/ppermute | solution.py:351
  83.7 5.8 %copy-start.8 = (s32[5]{0:T(128)S(1)}, s32[5]{0:T(128)}, u32[]{:S(2)}) copy-start(s32[5]{0:T(128)} %param.5) | copy-start | bytes 64
  83.8 6.3 %collective-permute-start.14 = (f32[1344,128]{1,0:T(8,128)S(1)}, f32[1344,128]{1,0:T(8,128)}, u32[]{:S(2)}, u32[]{:S(2)}) collective-permute-start(f32[1344,128]{1,0:T(8,128)S(1)} %pad_maximum_fusion.1.near_b), channel_id=1, source_target_pairs={{0,2},{2,0},{4,6},{6,4},{8,10},{10,8},{12,14},{14,12},{16,18},{18,... | collective-permute-start | bytes 2064392 | tf_op jit(solution)/shard_map/ppermute | solution.py:351
  88.0 2.5 %collective-permute-start.13 = (f32[1344,128]{1,0:T(8,128)}, f32[1344,128]{1,0:T(8,128)}, u32[]{:S(2)}, u32[]{:S(2)}) collective-permute-start(f32[1344,128]{1,0:T(8,128)} %pad_maximum_fusion.near_a), channel_id=1, source_target_pairs={{0,2},{2,0},{4,6},{6,4},{8,10},{10,8},{12,14},{14,12},{16,18},{18,... | collective-permute-start | bytes 2064392 | tf_op jit(solution)/shard_map/ppermute | solution.py:351
  88.0 47.8 %collective-permute-start.17 = (bf16[960,1024]{1,0:T(8,128)(2,1)}, bf16[960,1024]{1,0:T(8,128)(2,1)}, u32[]{:S(2)}, u32[]{:S(2)}) collective-permute-start(bf16[960,1024]{1,0:T(8,128)(2,1)} %get-tuple-element.14), channel_id=1, source_target_pairs={{0,1},{1,0},{2,3},{3,2},{4,5},{5,4},{6,7},{7,6},{8,9},{9,8},{10,11... | collective-permute-start | bytes 5898248 | tf_op jit(solution)/shard_map/ppermute | solution.py:437
  90.1 44.2 %copy-start = (bf16[1088,1024]{1,0:T(8,128)(2,1)}, bf16[1088,1024]{1,0:T(8,128)(2,1)S(1)}, u32[]{:S(2)}) copy-start(bf16[1088,1024]{1,0:T(8,128)(2,1)S(1)} %collective-permute-done.15.refs_0_) | copy-start | bytes 6684676
  134.3 5.7 %copy-start.3 = (bf16[64,1024]{1,0:T(8,128)(2,1)}, bf16[64,1024]{1,0:T(8,128)(2,1)S(1)}, u32[]{:S(2)}) copy-start(bf16[64,1024]{1,0:T(8,128)(2,1)S(1)} %get-tuple-element.13.near_ref) | copy-start | bytes 393220
  134.4 29.0 %copy-start.4 = (f32[8,1024]{1,0:T(8,128)}, f32[8,1024]{1,0:T(8,128)S(1)}, u32[]{:S(2)}) copy-start(f32[8,1024]{1,0:T(8,128)S(1)} %get-tuple-element.15.mean_ref) | copy-start | bytes 98308
  134.4 9.5 %copy-start.2 = (bf16[4096,64]{0,1:T(8,128)(2,1)S(1)}, bf16[4096,64]{0,1:T(8,128)(2,1)}, u32[]{:S(2)}) copy-start(bf16[4096,64]{0,1:T(8,128)(2,1)} %param.4) | copy-start | bytes 1572868
  134.4 5.6 %collective-permute-start.16 = (bf16[64,1024]{1,0:T(8,128)(2,1)S(1)}, bf16[64,1024]{1,0:T(8,128)(2,1)S(1)}, u32[]{:S(2)}, u32[]{:S(2)}) collective-permute-start(bf16[64,1024]{1,0:T(8,128)(2,1)S(1)} %get-tuple-element.13.near_ref), channel_id=1, source_target_pairs={{0,1},{1,0},{2,3},{3,2},{4,5},{5,4},{6,7},{7,6},{8,9},{9,8},{10,11... | collective-permute-start | bytes 393224 | tf_op jit(solution)/shard_map/ppermute | solution.py:447
  140.0 0.7 copy-start.6
  142.4 4.0 %collective-permute-start.18 = (f32[8,1024]{1,0:T(8,128)S(1)}, f32[8,1024]{1,0:T(8,128)S(1)}, u32[]{:S(2)}, u32[]{:S(2)}) collective-permute-start(f32[8,1024]{1,0:T(8,128)S(1)} %get-tuple-element.15.mean_ref), channel_id=1, source_target_pairs={{0,1},{1,0},{2,3},{3,2},{4,5},{5,4},{6,7},{7,6},{8,9},{9,8},{10,11... | collective-permute-start | bytes 98312 | tf_op jit(solution)/shard_map/ppermute | solution.py:448
  146.4 17.0 %copy-start.7 = (f32[8,1024]{1,0:T(8,128)}, f32[8,1024]{1,0:T(8,128)S(1)}, u32[]{:S(2)}) copy-start(f32[8,1024]{1,0:T(8,128)S(1)} %collective-permute-done.18.far_mean_ref) | copy-start | bytes 98308
  174.1 3.7 %collective-permute-start.19 = (f32[32,128]{1,0:T(8,128)S(1)}, f32[32,128]{1,0:T(8,128)S(1)}, u32[]{:S(2)}, u32[]{:S(2)}) collective-permute-start(f32[32,128]{1,0:T(8,128)S(1)} %constant_dynamic-slice_fusion), channel_id=1, source_target_pairs={{0,1},{1,0},{2,3},{3,2},{4,5},{5,4},{6,7},{7,6},{8,9},{9,8},{10,11... | collective-permute-start | bytes 49160 | tf_op jit(solution)/shard_map/ppermute | solution.py:455
  178.5 1.2 collective-permute-start.20
  179.7 3.7 %collective-permute-start.21 = (f32[32,128]{1,0:T(8,128)S(1)}, f32[32,128]{1,0:T(8,128)S(1)}, u32[]{:S(2)}, u32[]{:S(2)}) collective-permute-start(f32[32,128]{1,0:T(8,128)S(1)} %add.119), channel_id=1, source_target_pairs={{0,4},{2,6},{4,0},{6,2},{8,12},{10,14},{12,8},{14,10},{16,20},{18,... | collective-permute-start | bytes 49160 | tf_op jit(solution)/shard_map/ppermute | solution.py:351
  183.5 3.7 %collective-permute-start.22 = (f32[32,128]{1,0:T(8,128)S(1)}, f32[32,128]{1,0:T(8,128)S(1)}, u32[]{:S(2)}, u32[]{:S(2)}) collective-permute-start(f32[32,128]{1,0:T(8,128)S(1)} %add.120), channel_id=1, source_target_pairs={{0,8},{2,10},{4,12},{6,14},{8,0},{10,2},{12,4},{14,6},{16,24},{18,... | collective-permute-start | bytes 49160 | tf_op jit(solution)/shard_map/ppermute | solution.py:351
  187.2 4.6 %collective-permute-start.23 = (f32[32,128]{1,0:T(8,128)S(1)}, f32[32,128]{1,0:T(8,128)S(1)}, u32[]{:S(2)}, u32[]{:S(2)}) collective-permute-start(f32[32,128]{1,0:T(8,128)S(1)} %add.121), channel_id=1, source_target_pairs={{0,16},{2,18},{4,20},{6,22},{8,24},{10,26},{12,28},{14,30},{16,0},... | collective-permute-start | bytes 49160 | tf_op jit(solution)/shard_map/ppermute | solution.py:351
Sparse Core Ops, SparseCore 0:
  142.5 20.8 all-gather.2
where the time goes:
time: 204 us; the launch traced here: 200 us
  waiting for transfers between devices  73.1 us (36%)
  Pallas kernels  72 us (35%)
  starting transfers between devices  29.9 us (15%)
  between operations  14.5 us (7%)
  local copies, waits for them, and re-layouts  6.26 us (3%)
  other arithmetic  4.63 us (2%)
    ppermute x19, waiting for transfers between devices, swapped(): lax.ppermute(x, 'samp', [(i, i ^ 1 << bit) for i in range(lax.axis_size('...  48.1 us
    pallas_call x1, Pallas kernels, solve(): pl.pallas_call(functools.partial(solve_kernel, nsamp, ntraits), out_shape...  43.8 us
    ppermute x19, starting transfers between devices, swapped(): lax.ppermute(x, 'samp', [(i, i ^ 1 << bit) for i in range(lax.axis_size('...  22.2 us
    all_gather x1, waiting for transfers between devices, local(): coefs = lax.all_gather(both, 'samp', axis_index_groups=groups)  17 us
    pallas_call x1, Pallas kernels, gram(): pl.pallas_call(functools.partial(gram_kernel, ntraits), grid_spec=pltpu.P...  16.6 us
    pallas_call x1, Pallas kernels, level_sums(): pl.pallas_call(functools.partial(level_kernel, npen), out_shape=jax.Shape...  9.99 us
    ppermute x1, waiting for transfers between devices, local(): coef_far = lax.ppermute(coef, 'blk', [(0, 1), (1, 0)])  4.1 us
  transfers between devices with their start and end apart: 25, of which 20 were waited for; matrix products, arithmetic and copies ran while one was open for 2% of the time, Pallas kernels for 22%

commit v1 on v0

--- a/solution.py
+++ b/solution.py
@@ -58,6 +58,16 @@
 def as_right(x, axis):
     a, b, c = split(x)
     return jnp.concatenate([a, b, a, c, b, a], axis=axis)
+
+
+def stack_left(x):
+    a, b, c = [part.astype(jnp.float32) for part in split(x)]
+    return jnp.concatenate([a, a, b, a, b, c], axis=0).astype(jnp.bfloat16)
+
+
+def stack_right(x):
+    a, b, c = [part.astype(jnp.float32) for part in split(x)]
+    return jnp.concatenate([a, b, a, c, b, a], axis=0).astype(jnp.bfloat16)
 
 
 def invert_tile(tile):
@@ -80,15 +90,19 @@
 
             cols = cols[:j + 1] + [move(c) for c in cols[j + 1:]]
             right = move(right)
-        tops = [jnp.broadcast_to(right[j:j + 1, :], (SUB, BLK)) for j in range(SUB)]
+        mirror = jnp.where(lane < at, -strips[k], jnp.where(inside, 0.0, strips[k]))
+        change = lax.dot_general(stack_left(mirror), stack_right(right), TN, preferred_element_type=jnp.float32)
         fresh = []
         for i in range(BLK // SUB):
+            rest = jnp.where(inside, 0.0, strips[i])
             if i == k:
-                fresh.append(right)
-                continue
-            rest = jnp.where(inside, 0.0, strips[i])
-            for j in range(SUB):
-                rest = rest - jnp.broadcast_to(strips[i][:, at + j:at + j + 1], (SUB, BLK)) * tops[j]
+                rest = right
+            elif i == k + 1:
+                for j in range(SUB):
+                    factor = jnp.broadcast_to(strips[i][:, at + j:at + j + 1], (SUB, BLK))
+                    rest = rest - factor * jnp.broadcast_to(right[j:j + 1, :], (SUB, BLK))
+            else:
+                rest = rest - change[SUB * i:SUB * (i + 1), :]
             fresh.append(rest)
         strips = fresh
     return jnp.concatenate(strips, axis=0)
@@ -115,6 +129,15 @@
     dosage = geno_ref[...].astype(jnp.float32).astype(jnp.bfloat16)
 
     count = dosage.shape[0]
+    for j, panel in enumerate(panels):
+        left, right = dosage[:, wide * j:], dosage[:, wide * j:wide * (j + 1)]
+        panel[...] += lax.dot_general(left, right, TN, preferred_element_type=jnp.float32)
+    traits = traits_ref[...]
+    rows = jnp.concatenate([traits, jnp.ones((2 * SUB, count), jnp.bfloat16)], axis=0)
+    sums = jnp.dot(rows, dosage, preferred_element_type=jnp.float32)
+    side[...] += sums[0:side.shape[0], :]
+    ysum[...] += jnp.sum(traits.astype(jnp.float32), axis=1, keepdims=True)
+
     for tile in range(piece_starts(geno_ref.shape[0] * 2)[-1] // count):
         @pl.when(step == tile)
         def _(tile=tile):
@@ -127,15 +150,6 @@
     @pl.when(step >= half)
     def _():
         kept_ref[...] = dosage
-
-    for j, panel in enumerate(panels):
-        left, right = dosage[:, wide * j:], dosage[:, wide * j:wide * (j + 1)]
-        panel[...] += lax.dot_general(left, right, TN, preferred_element_type=jnp.float32)
-    traits = traits_ref[...]
-    rows = jnp.concatenate([traits, jnp.ones((2 * SUB, count), jnp.bfloat16)], axis=0)
-    sums = jnp.dot(rows, dosage, preferred_element_type=jnp.float32)
-    side[...] += sums[0:side.shape[0], :]
-    ysum[...] += jnp.sum(traits.astype(jnp.float32), axis=1, keepdims=True)
 
     def hand_out(even, odd):
         rows = even.shape[0]
@@ -452,8 +466,8 @@
     found = level_sums(kept, others, coefs, mean, mean_far, rows, npen)
     stack = nblk * npen
     each = ntraits // nblk
-    far = lax.ppermute(lax.dynamic_slice_in_dim(found, (1 - blk_rank) * each, each, 0), "blk", [(0, 1), (1, 0)])
-    found = small_sum(lax.dynamic_slice_in_dim(found, blk_rank * each, each, 0) + far) / nvars
+    found = small_sum(found + lax.ppermute(found, "blk", [(0, 1), (1, 0)]))
+    found = lax.dynamic_slice_in_dim(found, blk_rank * each, each, 0) / nvars
     return found[:, :stack * stack].reshape(each, stack, stack), found[:, stack * stack:stack * stack + stack]
 
 

time: 204 us -> 197 us (0.966); the launches traced: 200 us -> 196 us
  Pallas kernels: 72 us -> 67.9 us
    pallas_call x1, Pallas kernels: 43.8 us -> 41.5 us  [solve(): pl.pallas_call(functools.partial(solve_kernel, nsamp, ntraits), out_shape...]
  transfers between devices with their start and end apart: 25 -> 25, of which waited for: 20 -> 20; matrix products, arithmetic and copies ran while one was open for 2% -> 2% of each run, Pallas kernels for 22% -> 21%
where the time goes in v1:
time: 197 us; the launch traced here: 196 us
  waiting for transfers between devices  74 us (38%)
  Pallas kernels  67.9 us (34%)
  starting transfers between devices  29.8 us (15%)
  between operations  14.3 us (7%)
  local copies, waits for them, and re-layouts  5.54 us (3%)
  other arithmetic  4.68 us (2%)
    ppermute x19, waiting for transfers between devices, swapped(): lax.ppermute(x, 'samp', [(i, i ^ 1 << bit) for i in range(lax.axis_size('...  48.7 us
    pallas_call x1, Pallas kernels, solve(): pl.pallas_call(functools.partial(solve_kernel, nsamp, ntraits), out_shape...  41.5 us
    ppermute x19, starting transfers between devices, swapped(): lax.ppermute(x, 'samp', [(i, i ^ 1 << bit) for i in range(lax.axis_size('...  22.1 us
    all_gather x1, waiting for transfers between devices, local(): coefs = lax.all_gather(both, 'samp', axis_index_groups=groups)  17 us
    pallas_call x1, Pallas kernels, gram(): pl.pallas_call(functools.partial(gram_kernel, ntraits), grid_spec=pltpu.P...  14.7 us
    pallas_call x1, Pallas kernels, level_sums(): pl.pallas_call(functools.partial(level_kernel, npen), out_shape=jax.Shape...  9.99 us
    ppermute x1, waiting for transfers between devices, local(): coef_far = lax.ppermute(coef, 'blk', [(0, 1), (1, 0)])  4.07 us
  transfers between devices with their start and end apart: 25, of which 20 were waited for; matrix products, arithmetic and copies ran while one was open for 2% of the time, Pallas kernels for 21%

profile of v1, /device:TPU:0, one launch (start us, length us, event | category | flops | bytes accessed | tf_op | source)
XLA Modules:
  0.0 196.2 jit_solution(5175665055681158966)
XLA Ops:
  7.3 1.0 copy-done.1
  8.3 14.7 %gram_sums.1 = (f32[2688,128]{1,0:T(8,128)S(1)}, f32[2688,128]{1,0:T(8,128)S(1)}, bf16[2048,1024]{1,0:T(8,128)(2,1)}, bf16[1088,1024]{1,0:T(8,128)(2,1)}, bf16[960,1024]{1,0:T(8,128)(2,1)}) custom-call(s32[2]{0:T(128)S(1)} %pad_add_fusion.rank_ref, s32[4096,1024]{1,0:T(8,128)} %geno_ref.1, bf16[64,4096]{1,0:T(8,128)(2,1)S(1)} %bitcast.10), custom_call_target="tpu_custom_call" | custom-call | tf_op jit(solution)/shard_map/gram_sums/pallas_call | solution.py:205
  23.4 2.9 %collective-permute-done = f32[2688,128]{1,0:T(8,128)} collective-permute-done((f32[2688,128]{1,0:T(8,128)S(1)}, f32[2688,128]{1,0:T(8,128)}, u32[]{:S(2)}, u32[]{:S(2)}) %collective-permute-start) | collective-permute-done | bytes 1376288 | tf_op jit(solution)/shard_map/ppermute | solution.py:365
  26.3 1.5 add.93
  27.9 0.8 constant_dynamic-slice_fusion.2
  28.7 3.0 %collective-permute-start.7 = (f32[672,128]{1,0:T(8,128)}, f32[672,128]{1,0:T(8,128)S(1)}, u32[]{:S(2)}, u32[]{:S(2)}) collective-permute-start(f32[672,128]{1,0:T(8,128)} %constant_dynamic-slice_fusion.2), channel_id=1, source_target_pairs={{0,8},{2,10},{4,12},{6,14},{8,0},{10,2},{12,4},{14,6},{16,24},{18,... | collective-permute-start | bytes 1032200 | tf_op jit(solution)/shard_map/ppermute | solution.py:365
  31.7 1.5 collective-permute-start.15
  33.2 1.6 collective-permute-start.1
  34.8 5.5 %collective-permute-done.7 = f32[672,128]{1,0:T(8,128)S(1)} collective-permute-done((f32[672,128]{1,0:T(8,128)}, f32[672,128]{1,0:T(8,128)S(1)}, u32[]{:S(2)}, u32[]{:S(2)}) %collective-permute-start.7) | collective-permute-done | bytes 344096 | tf_op jit(solution)/shard_map/ppermute | solution.py:365
  40.3 1.0 dynamic-slice_add_fusion
  41.3 2.8 %collective-permute-start.8 = (f32[336,128]{1,0:T(8,128)S(1)}, f32[336,128]{1,0:T(8,128)S(1)}, u32[]{:S(2)}, u32[]{:S(2)}) collective-permute-start(f32[336,128]{1,0:T(8,128)S(1)} %constant_dynamic-slice_fusion.1), channel_id=1, source_target_pairs={{0,16},{2,18},{4,20},{6,22},{8,24},{10,26},{12,28},{14,30},{16,0},... | collective-permute-start | bytes 516104 | tf_op jit(solution)/shard_map/ppermute | solution.py:365
  44.2 1.6 collective-permute-start.2
  45.8 6.1 %collective-permute-done.8 = f32[336,128]{1,0:T(8,128)S(1)} collective-permute-done((f32[336,128]{1,0:T(8,128)S(1)}, f32[336,128]{1,0:T(8,128)S(1)}, u32[]{:S(2)}, u32[]{:S(2)}) %collective-permute-start.8) | collective-permute-done | bytes 172064 | tf_op jit(solution)/shard_map/ppermute | solution.py:365
  52.0 1.4 collective-permute-start.9
  53.5 0.6 collective-permute-start.3
  54.1 2.4 %collective-permute-done.9 = f32[168,128]{1,0:T(8,128)S(1)} collective-permute-done((f32[168,128]{1,0:T(8,128)S(1)}, f32[168,128]{1,0:T(8,128)S(1)}, u32[]{:S(2)}, u32[]{:S(2)}) %collective-permute-start.9) | collective-permute-done | bytes 86048 | tf_op jit(solution)/shard_map/ppermute | solution.py:365
  56.6 1.4 collective-permute-start.10
  58.0 2.9 %collective-permute-done.3 = f32[168,128]{1,0:T(8,128)S(1)} collective-permute-done((f32[168,128]{1,0:T(8,128)S(1)}, f32[168,128]{1,0:T(8,128)S(1)}, u32[]{:S(2)}, u32[]{:S(2)}) %collective-permute-start.3) | collective-permute-done | bytes 86048 | tf_op jit(solution)/shard_map/ppermute | solution.py:365
  61.2 2.9 %collective-permute-start.11 = (f32[336,128]{1,0:T(8,128)S(1)}, f32[336,128]{1,0:T(8,128)S(1)}, u32[]{:S(2)}, u32[]{:S(2)}) collective-permute-start(f32[336,128]{1,0:T(8,128)S(1)} %pad_maximum_fusion.5), channel_id=1, source_target_pairs={{0,16},{2,18},{4,20},{6,22},{8,24},{10,26},{12,28},{14,30},{16,0},... | collective-permute-start | bytes 516104 | tf_op jit(solution)/shard_map/ppermute | solution.py:365
  64.1 6.3 %collective-permute-done.4 = f32[168,128]{1,0:T(8,128)S(1)} collective-permute-done((f32[168,128]{1,0:T(8,128)S(1)}, f32[168,128]{1,0:T(8,128)S(1)}, u32[]{:S(2)}, u32[]{:S(2)}) %collective-permute-start.4) | collective-permute-done | bytes 86048 | tf_op jit(solution)/shard_map/ppermute | solution.py:365
  70.4 1.7 collective-permute-done.11
  72.6 5.1 %collective-permute-done.5 = f32[336,128]{1,0:T(8,128)S(1)} collective-permute-done((f32[336,128]{1,0:T(8,128)S(1)}, f32[336,128]{1,0:T(8,128)S(1)}, u32[]{:S(2)}, u32[]{:S(2)}) %collective-permute-start.5) | collective-permute-done | bytes 172064 | tf_op jit(solution)/shard_map/ppermute | solution.py:365
  77.9 3.9 %collective-permute-done.12 = f32[672,128]{1,0:T(8,128)S(1)} collective-permute-done((f32[672,128]{1,0:T(8,128)S(1)}, f32[672,128]{1,0:T(8,128)S(1)}, u32[]{:S(2)}, u32[]{:S(2)}) %collective-permute-start.12) | collective-permute-done | bytes 344096 | tf_op jit(solution)/shard_map/ppermute | solution.py:365
  82.0 3.1 %collective-permute-done.6 = f32[672,128]{1,0:T(8,128)S(1)} collective-permute-done((f32[672,128]{1,0:T(8,128)S(1)}, f32[672,128]{1,0:T(8,128)S(1)}, u32[]{:S(2)}, u32[]{:S(2)}) %collective-permute-start.6) | collective-permute-done | bytes 344096 | tf_op jit(solution)/shard_map/ppermute | solution.py:365
  85.2 0.9 pad_maximum_fusion.near_a
  86.1 1.5 collective-permute-start.17
  88.6 41.5 %ridge_solve.1 = (bf16[64,1024]{1,0:T(8,128)(2,1)S(1)}, f32[8,1024]{1,0:T(8,128)S(1)}) custom-call(f32[1,1]{1,0:T(1,128)} %bitcast.3.lam_ref, f32[1344,128]{1,0:T(8,128)} %pad_maximum_fusion.near_a, f32[1344,128]{1,0:T(8,128)S(1)} %pad_maximum_fusion.1.near_b, f32[1344,128]{1,0:T(8,128)} %collective-permute-done.13.far_a, ...), custom_call_target="tpu_custom_call" | custom-call | flops 46000001024 | bytes 1000000 | tf_op jit(solution)/shard_map/ridge_solve/pallas_call | solution.py:292
  130.1 1.5 collective-permute-start.16
  131.7 4.1 %collective-permute-done.16.far_ref = bf16[64,1024]{1,0:T(8,128)(2,1)S(1)} collective-permute-done((bf16[64,1024]{1,0:T(8,128)(2,1)S(1)}, bf16[64,1024]{1,0:T(8,128)(2,1)S(1)}, u32[]{:S(2)}, u32[]{:S(2)}) %collective-permute-start.16) | collective-permute-done | bytes 131104 | tf_op jit(solution)/shard_map/ppermute | solution.py:461
  135.7 0.6 copy-done.6
  136.4 1.7 stack_blocks.1
  138.1 1.5 collective-permute-start.18
  139.6 0.7 dynamic-slice_bitcast_fusion.traits_ref
  140.4 1.7 collective-permute-done.18.far_mean_ref
  142.1 17.0 %all-gather.3.cloned.1.call-done = bf16[16,64,1024]{2,1,0:T(8,128)(2,1)} async-done(((bf16[2,64,1024]{2,1,0:T(8,128)(2,1)}), bf16[16,64,1024]{2,1,0:T(8,128)(2,1)}) %all-gather.3.cloned.1.call-update) | async-done | bytes 2097168 | tf_op jit(solution)/shard_map/all_gather | solution.py:464
  159.1 10.0 %level_sums.1 = f32[64,128]{1,0:T(8,128)} custom-call(bf16[2048,1024]{1,0:T(8,128)(2,1)} %get-tuple-element.9.own_ref, bf16[8,2,64,1024]{3,2,1,0:T(8,128)(2,1)} %bitcast.11, f32[8,1024]{1,0:T(8,128)} %copy-done.4, f32[8,1024]{1,0:T(8,128)} %copy-done.7, bf16[64,2048]{1,0:T(8,128)(2,1)} %dynamic-slice_bitcast_fusion.traits_ref, bf16[1088,1024]{1,0:T(8,128)(2,1)} %copy-done, ...), custom_call_target="tpu_custom_call" | custom-call | tf_op jit(solution)/shard_map/level_sums/pallas_call | solution.py:350
  169.1 1.6 collective-permute-start.19
  170.8 2.5 %collective-permute-done.19 = f32[64,128]{1,0:T(8,128)S(1)} collective-permute-done((f32[64,128]{1,0:T(8,128)}, f32[64,128]{1,0:T(8,128)S(1)}, u32[]{:S(2)}, u32[]{:S(2)}) %collective-permute-start.19) | collective-permute-done | bytes 32800 | tf_op jit(solution)/shard_map/ppermute | solution.py:469
  173.3 0.8 add.113
  174.0 1.2 collective-permute-done.20
  175.2 1.5 collective-permute-start.21
  176.7 2.4 %collective-permute-done.21 = f32[64,128]{1,0:T(8,128)S(1)} collective-permute-done((f32[64,128]{1,0:T(8,128)S(1)}, f32[64,128]{1,0:T(8,128)S(1)}, u32[]{:S(2)}, u32[]{:S(2)}) %collective-permute-start.21) | collective-permute-done | bytes 32800 | tf_op jit(solution)/shard_map/ppermute | solution.py:365
  179.2 1.6 collective-permute-start.22
  180.7 2.3 %collective-permute-done.22 = f32[64,128]{1,0:T(8,128)S(1)} collective-permute-done((f32[64,128]{1,0:T(8,128)S(1)}, f32[64,128]{1,0:T(8,128)S(1)}, u32[]{:S(2)}, u32[]{:S(2)}) %collective-permute-start.22) | collective-permute-done | bytes 32800 | tf_op jit(solution)/shard_map/ppermute | solution.py:365
  183.1 2.6 %collective-permute-start.23 = (f32[64,128]{1,0:T(8,128)S(1)}, f32[64,128]{1,0:T(8,128)S(1)}, u32[]{:S(2)}, u32[]{:S(2)}) collective-permute-start(f32[64,128]{1,0:T(8,128)S(1)} %add.116), channel_id=1, source_target_pairs={{0,16},{2,18},{4,20},{6,22},{8,24},{10,26},{12,28},{14,30},{16,0},... | collective-permute-start | bytes 98312 | tf_op jit(solution)/shard_map/ppermute | solution.py:365
  185.7 2.2 %collective-permute-done.23 = f32[64,128]{1,0:T(8,128)S(1)} collective-permute-done((f32[64,128]{1,0:T(8,128)S(1)}, f32[64,128]{1,0:T(8,128)S(1)}, u32[]{:S(2)}, u32[]{:S(2)}) %collective-permute-start.23) | collective-permute-done | bytes 32800 | tf_op jit(solution)/shard_map/ppermute | solution.py:365
  188.1 0.6 reshape.11
  188.7 0.7 copy.10
  (64 shorter events, 3.1 us)
Async XLA Ops:
  7.2 152.0 %all-gather.3.cloned.1.call-start = ((), (), s32[]{:S(2)}) async-start(), calls=%async_computation | async-start | bytes 2359296 | tf_op jit(solution)/shard_map/all_gather | solution.py:464
  7.3 1.0 copy-start.1
  23.0 3.3 %collective-permute-start = (f32[2688,128]{1,0:T(8,128)S(1)}, f32[2688,128]{1,0:T(8,128)}, u32[]{:S(2)}, u32[]{:S(2)}) collective-permute-start(f32[2688,128]{1,0:T(8,128)S(1)} %get-tuple-element.11), channel_id=1, source_target_pairs={{0,2},{2,0},{4,6},{6,4},{8,10},{10,8},{12,14},{14,12},{16,18},{18,... | collective-permute-start | bytes 4128776 | tf_op jit(solution)/shard_map/ppermute | solution.py:365
  27.9 3.8 %copy-start.5 = (f32[1344,128]{1,0:T(8,128)}, f32[1344,128]{1,0:T(8,128)S(1)}, u32[]{:S(2)}) copy-start(f32[1344,128]{1,0:T(8,128)S(1)} %get-tuple-element.22) | copy-start | bytes 2064388
  28.7 11.5 %collective-permute-start.7 = (f32[672,128]{1,0:T(8,128)}, f32[672,128]{1,0:T(8,128)S(1)}, u32[]{:S(2)}, u32[]{:S(2)}) collective-permute-start(f32[672,128]{1,0:T(8,128)} %constant_dynamic-slice_fusion.2), channel_id=1, source_target_pairs={{0,8},{2,10},{4,12},{6,14},{8,0},{10,2},{12,4},{14,6},{16,24},{18,... | collective-permute-start | bytes 1032200 | tf_op jit(solution)/shard_map/ppermute | solution.py:365
  31.7 56.5 %collective-permute-start.15 = (bf16[1088,1024]{1,0:T(8,128)(2,1)}, bf16[1088,1024]{1,0:T(8,128)(2,1)S(1)}, u32[]{:S(2)}, u32[]{:S(2)}) collective-permute-start(bf16[1088,1024]{1,0:T(8,128)(2,1)} %get-tuple-element.12), channel_id=1, source_target_pairs={{0,1},{1,0},{2,3},{3,2},{4,5},{5,4},{6,7},{7,6},{8,9},{9,8},{10,11... | collective-permute-start | bytes 6684680 | tf_op jit(solution)/shard_map/ppermute | solution.py:451
  33.2 10.9 %collective-permute-start.1 = (f32[672,128]{1,0:T(8,128)S(1)}, f32[672,128]{1,0:T(8,128)S(1)}, u32[]{:S(2)}, u32[]{:S(2)}) collective-permute-start(f32[672,128]{1,0:T(8,128)S(1)} %constant_dynamic-slice_fusion.5), channel_id=1, source_target_pairs={{0,4},{2,6},{4,0},{6,2},{8,12},{10,14},{12,8},{14,10},{16,20},{18,... | collective-permute-start | bytes 1032200 | tf_op jit(solution)/shard_map/ppermute | solution.py:365
  41.3 10.7 %collective-permute-start.8 = (f32[336,128]{1,0:T(8,128)S(1)}, f32[336,128]{1,0:T(8,128)S(1)}, u32[]{:S(2)}, u32[]{:S(2)}) collective-permute-start(f32[336,128]{1,0:T(8,128)S(1)} %constant_dynamic-slice_fusion.1), channel_id=1, source_target_pairs={{0,16},{2,18},{4,20},{6,22},{8,24},{10,26},{12,28},{14,30},{16,0},... | collective-permute-start | bytes 516104 | tf_op jit(solution)/shard_map/ppermute | solution.py:365
  44.2 9.2 %collective-permute-start.2 = (f32[336,128]{1,0:T(8,128)S(1)}, f32[336,128]{1,0:T(8,128)S(1)}, u32[]{:S(2)}, u32[]{:S(2)}) collective-permute-start(f32[336,128]{1,0:T(8,128)S(1)} %constant_dynamic-slice_fusion.4), channel_id=1, source_target_pairs={{0,8},{2,10},{4,12},{6,14},{8,0},{10,2},{12,4},{14,6},{16,24},{18,... | collective-permute-start | bytes 516104 | tf_op jit(solution)/shard_map/ppermute | solution.py:365
  52.0 4.6 %collective-permute-start.9 = (f32[168,128]{1,0:T(8,128)S(1)}, f32[168,128]{1,0:T(8,128)S(1)}, u32[]{:S(2)}, u32[]{:S(2)}) collective-permute-start(f32[168,128]{1,0:T(8,128)S(1)} %constant_dynamic-slice_fusion), channel_id=1, source_target_pairs={{0,4},{2,6},{4,0},{6,2},{8,12},{10,14},{12,8},{14,10},{16,20},{18,... | collective-permute-start | bytes 258056 | tf_op jit(solution)/shard_map/ppermute | solution.py:365
  53.5 7.5 %collective-permute-start.3 = (f32[168,128]{1,0:T(8,128)S(1)}, f32[168,128]{1,0:T(8,128)S(1)}, u32[]{:S(2)}, u32[]{:S(2)}) collective-permute-start(f32[168,128]{1,0:T(8,128)S(1)} %constant_dynamic-slice_fusion.3), channel_id=1, source_target_pairs={{0,16},{2,18},{4,20},{6,22},{8,24},{10,26},{12,28},{14,30},{16,0},... | collective-permute-start | bytes 258056 | tf_op jit(solution)/shard_map/ppermute | solution.py:365
  56.6 4.6 %collective-permute-start.10 = (f32[168,128]{1,0:T(8,128)S(1)}, f32[168,128]{1,0:T(8,128)S(1)}, u32[]{:S(2)}, u32[]{:S(2)}) collective-permute-start(f32[168,128]{1,0:T(8,128)S(1)} %dynamic-slice_add_fusion.4), channel_id=1, source_target_pairs={{0,4},{2,6},{4,0},{6,2},{8,12},{10,14},{12,8},{14,10},{16,20},{18,... | collective-permute-start | bytes 258056 | tf_op jit(solution)/shard_map/ppermute | solution.py:365
  61.0 9.4 %collective-permute-start.4 = (f32[168,128]{1,0:T(8,128)S(1)}, f32[168,128]{1,0:T(8,128)S(1)}, u32[]{:S(2)}, u32[]{:S(2)}) collective-permute-start(f32[168,128]{1,0:T(8,128)S(1)} %dynamic-slice_add_fusion.5), channel_id=1, source_target_pairs={{0,16},{2,18},{4,20},{6,22},{8,24},{10,26},{12,28},{14,30},{16,0},... | collective-permute-start | bytes 258056 | tf_op jit(solution)/shard_map/ppermute | solution.py:365
  61.2 11.0 %collective-permute-start.11 = (f32[336,128]{1,0:T(8,128)S(1)}, f32[336,128]{1,0:T(8,128)S(1)}, u32[]{:S(2)}, u32[]{:S(2)}) collective-permute-start(f32[336,128]{1,0:T(8,128)S(1)} %pad_maximum_fusion.5), channel_id=1, source_target_pairs={{0,16},{2,18},{4,20},{6,22},{8,24},{10,26},{12,28},{14,30},{16,0},... | collective-permute-start | bytes 516104 | tf_op jit(solution)/shard_map/ppermute | solution.py:365
  70.4 7.4 %collective-permute-start.5 = (f32[336,128]{1,0:T(8,128)S(1)}, f32[336,128]{1,0:T(8,128)S(1)}, u32[]{:S(2)}, u32[]{:S(2)}) collective-permute-start(f32[336,128]{1,0:T(8,128)S(1)} %pad_maximum_fusion.4), channel_id=1, source_target_pairs={{0,8},{2,10},{4,12},{6,14},{8,0},{10,2},{12,4},{14,6},{16,24},{18,... | collective-permute-start | bytes 516104 | tf_op jit(solution)/shard_map/ppermute | solution.py:365
  72.2 9.6 %collective-permute-start.12 = (f32[672,128]{1,0:T(8,128)S(1)}, f32[672,128]{1,0:T(8,128)S(1)}, u32[]{:S(2)}, u32[]{:S(2)}) collective-permute-start(f32[672,128]{1,0:T(8,128)S(1)} %pad_maximum_fusion.3), channel_id=1, source_target_pairs={{0,8},{2,10},{4,12},{6,14},{8,0},{10,2},{12,4},{14,6},{16,24},{18,... | collective-permute-start | bytes 1032200 | tf_op jit(solution)/shard_map/ppermute | solution.py:365
  77.8 7.3 %collective-permute-start.6 = (f32[672,128]{1,0:T(8,128)S(1)}, f32[672,128]{1,0:T(8,128)S(1)}, u32[]{:S(2)}, u32[]{:S(2)}) collective-permute-start(f32[672,128]{1,0:T(8,128)S(1)} %pad_maximum_fusion.2), channel_id=1, source_target_pairs={{0,4},{2,6},{4,0},{6,2},{8,12},{10,14},{12,8},{14,10},{16,20},{18,... | collective-permute-start | bytes 1032200 | tf_op jit(solution)/shard_map/ppermute | solution.py:365
  81.8 5.7 %copy-start.8 = (s32[5]{0:T(128)S(1)}, s32[5]{0:T(128)}, u32[]{:S(2)}) copy-start(s32[5]{0:T(128)} %param.5) | copy-start | bytes 64
  81.9 6.3 %collective-permute-start.14 = (f32[1344,128]{1,0:T(8,128)S(1)}, f32[1344,128]{1,0:T(8,128)}, u32[]{:S(2)}, u32[]{:S(2)}) collective-permute-start(f32[1344,128]{1,0:T(8,128)S(1)} %pad_maximum_fusion.1.near_b), channel_id=1, source_target_pairs={{0,2},{2,0},{4,6},{6,4},{8,10},{10,8},{12,14},{14,12},{16,18},{18,... | collective-permute-start | bytes 2064392 | tf_op jit(solution)/shard_map/ppermute | solution.py:365
  86.1 2.5 %collective-permute-start.13 = (f32[1344,128]{1,0:T(8,128)}, f32[1344,128]{1,0:T(8,128)}, u32[]{:S(2)}, u32[]{:S(2)}) collective-permute-start(f32[1344,128]{1,0:T(8,128)} %pad_maximum_fusion.near_a), channel_id=1, source_target_pairs={{0,2},{2,0},{4,6},{6,4},{8,10},{10,8},{12,14},{14,12},{16,18},{18,... | collective-permute-start | bytes 2064392 | tf_op jit(solution)/shard_map/ppermute | solution.py:365
  86.1 45.6 %collective-permute-start.17 = (bf16[960,1024]{1,0:T(8,128)(2,1)}, bf16[960,1024]{1,0:T(8,128)(2,1)}, u32[]{:S(2)}, u32[]{:S(2)}) collective-permute-start(bf16[960,1024]{1,0:T(8,128)(2,1)} %get-tuple-element.14), channel_id=1, source_target_pairs={{0,1},{1,0},{2,3},{3,2},{4,5},{5,4},{6,7},{7,6},{8,9},{9,8},{10,11... | collective-permute-start | bytes 5898248 | tf_op jit(solution)/shard_map/ppermute | solution.py:451
  88.2 41.9 %copy-start = (bf16[1088,1024]{1,0:T(8,128)(2,1)}, bf16[1088,1024]{1,0:T(8,128)(2,1)S(1)}, u32[]{:S(2)}) copy-start(bf16[1088,1024]{1,0:T(8,128)(2,1)S(1)} %collective-permute-done.15.refs_0_) | copy-start | bytes 6684676
  130.1 5.6 %copy-start.3 = (bf16[64,1024]{1,0:T(8,128)(2,1)}, bf16[64,1024]{1,0:T(8,128)(2,1)S(1)}, u32[]{:S(2)}) copy-start(bf16[64,1024]{1,0:T(8,128)(2,1)S(1)} %get-tuple-element.13.near_ref) | copy-start | bytes 393220
  130.1 29.0 %copy-start.4 = (f32[8,1024]{1,0:T(8,128)}, f32[8,1024]{1,0:T(8,128)S(1)}, u32[]{:S(2)}) copy-start(f32[8,1024]{1,0:T(8,128)S(1)} %get-tuple-element.15.mean_ref) | copy-start | bytes 98308
  130.1 9.5 %copy-start.2 = (bf16[4096,64]{0,1:T(8,128)(2,1)S(1)}, bf16[4096,64]{0,1:T(8,128)(2,1)}, u32[]{:S(2)}) copy-start(bf16[4096,64]{0,1:T(8,128)(2,1)} %param.4) | copy-start | bytes 1572868
  130.1 5.6 %collective-permute-start.16 = (bf16[64,1024]{1,0:T(8,128)(2,1)S(1)}, bf16[64,1024]{1,0:T(8,128)(2,1)S(1)}, u32[]{:S(2)}, u32[]{:S(2)}) collective-permute-start(bf16[64,1024]{1,0:T(8,128)(2,1)S(1)} %get-tuple-element.13.near_ref), channel_id=1, source_target_pairs={{0,1},{1,0},{2,3},{3,2},{4,5},{5,4},{6,7},{7,6},{8,9},{9,8},{10,11... | collective-permute-start | bytes 393224 | tf_op jit(solution)/shard_map/ppermute | solution.py:461
  135.7 0.7 copy-start.6
  138.1 4.0 %collective-permute-start.18 = (f32[8,1024]{1,0:T(8,128)S(1)}, f32[8,1024]{1,0:T(8,128)S(1)}, u32[]{:S(2)}, u32[]{:S(2)}) collective-permute-start(f32[8,1024]{1,0:T(8,128)S(1)} %get-tuple-element.15.mean_ref), channel_id=1, source_target_pairs={{0,1},{1,0},{2,3},{3,2},{4,5},{5,4},{6,7},{7,6},{8,9},{9,8},{10,11... | collective-permute-start | bytes 98312 | tf_op jit(solution)/shard_map/ppermute | solution.py:462
  142.1 17.0 %copy-start.7 = (f32[8,1024]{1,0:T(8,128)}, f32[8,1024]{1,0:T(8,128)S(1)}, u32[]{:S(2)}) copy-start(f32[8,1024]{1,0:T(8,128)S(1)} %collective-permute-done.18.far_mean_ref) | copy-start | bytes 98308
  169.1 4.1 %collective-permute-start.19 = (f32[64,128]{1,0:T(8,128)}, f32[64,128]{1,0:T(8,128)S(1)}, u32[]{:S(2)}, u32[]{:S(2)}) collective-permute-start(f32[64,128]{1,0:T(8,128)} %level_sums.1), channel_id=1, source_target_pairs={{0,1},{1,0},{2,3},{3,2},{4,5},{5,4},{6,7},{7,6},{8,9},{9,8},{10,11... | collective-permute-start | bytes 98312 | tf_op jit(solution)/shard_map/ppermute | solution.py:469
  174.0 1.2 collective-permute-start.20
  175.2 3.9 %collective-permute-start.21 = (f32[64,128]{1,0:T(8,128)S(1)}, f32[64,128]{1,0:T(8,128)S(1)}, u32[]{:S(2)}, u32[]{:S(2)}) collective-permute-start(f32[64,128]{1,0:T(8,128)S(1)} %add.114), channel_id=1, source_target_pairs={{0,4},{2,6},{4,0},{6,2},{8,12},{10,14},{12,8},{14,10},{16,20},{18,... | collective-permute-start | bytes 98312 | tf_op jit(solution)/shard_map/ppermute | solution.py:365
  179.2 3.9 %collective-permute-start.22 = (f32[64,128]{1,0:T(8,128)S(1)}, f32[64,128]{1,0:T(8,128)S(1)}, u32[]{:S(2)}, u32[]{:S(2)}) collective-permute-start(f32[64,128]{1,0:T(8,128)S(1)} %add.115), channel_id=1, source_target_pairs={{0,8},{2,10},{4,12},{6,14},{8,0},{10,2},{12,4},{14,6},{16,24},{18,... | collective-permute-start | bytes 98312 | tf_op jit(solution)/shard_map/ppermute | solution.py:365
  183.1 4.8 %collective-permute-start.23 = (f32[64,128]{1,0:T(8,128)S(1)}, f32[64,128]{1,0:T(8,128)S(1)}, u32[]{:S(2)}, u32[]{:S(2)}) collective-permute-start(f32[64,128]{1,0:T(8,128)S(1)} %add.116), channel_id=1, source_target_pairs={{0,16},{2,18},{4,20},{6,22},{8,24},{10,26},{12,28},{14,30},{16,0},... | collective-permute-start | bytes 98312 | tf_op jit(solution)/shard_map/ppermute | solution.py:365
Sparse Core Ops, SparseCore 0:
  138.2 20.8 all-gather.2

commit v2 on v1

--- a/solution.py
+++ b/solution.py
@@ -109,7 +109,7 @@
 
 
 def piece_starts(rows):
-    return [0, rows * 17 // 32, rows]
+    return [0, rows // 2, rows]
 
 
 def gram_kernel(ntraits, rank_ref, geno_ref, traits_ref, near_ref, away_ref, kept_ref, *refs):
@@ -191,7 +191,7 @@
     tile = count // steps
     half = steps // 2
     low = panel_rows(nvars)[1]
-    share = 2 * SUB * members
+    share = SUB * members
     total = -(-(low + side_rows(ntraits) * (nvars // BLK) + ntraits) // share) * share
 
     def source(i, place_ref):
@@ -224,7 +224,7 @@
     )(place, genotypes, traits)
 
 
-def solve_kernel(nsamp, ntraits, lam_ref, near_a, near_b, far_a, far_b, *refs):
+def solve_kernel(nsamp, ntraits, lam_ref, near, far, *refs):
     coef_ref, mean_ref, aug, wide = refs[-4:]
     nvars = coef_ref.shape[1]
     nblocks = nvars // BLK
@@ -232,14 +232,14 @@
     tall = side_rows(ntraits)
     lam = lam_ref[0, 0]
     lower = lax.rem(lax.axis_index("samp"), 2) == 0
-    quarter = near_a.shape[0]
-    pairs = [(near_a, far_a), (near_b, far_b), (far_a, near_a), (far_b, near_b)]
+    half = near.shape[0]
+    pairs = [(near, far), (far, near)]
 
     def read(row, count):
         found = []
         while count > 0:
-            place, at = divmod(row, quarter)
-            size = min(count, quarter - at)
+            place, at = divmod(row, half)
+            size = min(count, half - at)
             even, odd = pairs[place]
             found.append(jnp.where(lower, even[at:at + size, :], odd[at:at + size, :]))
             row, count = row + size, count - size
@@ -293,7 +293,7 @@
         functools.partial(solve_kernel, nsamp, ntraits),
         out_shape=[jax.ShapeDtypeStruct((ntraits, nvars), jnp.bfloat16), jax.ShapeDtypeStruct((SUB, nvars), jnp.float32)],
         in_specs=[pl.BlockSpec(memory_space=pltpu.SMEM)]
-        + [pl.BlockSpec(memory_space=pltpu.VMEM)] * 4
+        + [pl.BlockSpec(memory_space=pltpu.VMEM)] * 2
         + [pl.BlockSpec(memory_space=pl.ANY)] * len(arrived),
         out_specs=[pl.BlockSpec(memory_space=pltpu.VMEM)] * 2,
         scratch_shapes=[
@@ -313,21 +313,20 @@
     count = own_ref.shape[0]
     stack = 2 * npen
     tile = 512
-    pieces, (out_ref, pred, other_ref) = refs[:-3], refs[-3:]
-    low = 0
-    for piece in pieces:
-        other_ref[low:low + piece.shape[0], :] = piece[...]
-        low += piece.shape[0]
+    pieces, (out_ref, pred) = refs[:-2], refs[-2:]
     for place in range(2):
         block = rank if place == 0 else 1 - rank
-        source = own_ref if place == 0 else other_ref
+        sources = [own_ref] if place == 0 else pieces
         mean = (mean_ref if place == 0 else far_mean_ref)[0:1, :]
         coef = jnp.concatenate([coef_ref[r, block] for r in range(npen)], axis=0)
         offset = jnp.sum(coef.astype(jnp.float32) * mean, axis=1, keepdims=True)
         low = pl.multiple_of(block * (npen * ntraits), npen * ntraits)
-        for n in range(0, count, tile):
-            value = lax.dot_general(coef, source[n:n + tile, :], NT, preferred_element_type=jnp.float32)
-            pred[pl.ds(low, npen * ntraits), n:n + tile] = value - offset
+        n = 0
+        for source in sources:
+            for first in range(0, source.shape[0], tile):
+                value = lax.dot_general(coef, source[first:first + tile, :], NT, preferred_element_type=jnp.float32)
+                pred[pl.ds(low, npen * ntraits), n:n + tile] = value - offset
+                n += tile
     pred[stack * ntraits:(stack + 1) * ntraits, :] = traits_ref[...].astype(jnp.float32)
     lane = lax.broadcasted_iota(jnp.int32, (SUB, BLK), 1)
     for t in range(0, ntraits, SUB):
@@ -354,19 +353,20 @@
         out_specs=pl.BlockSpec(memory_space=pltpu.VMEM),
         scratch_shapes=[
             pltpu.VMEM(((2 * npen + 1) * ntraits, count), jnp.float32),
-            pltpu.VMEM(own.shape, own.dtype),
         ],
         compiler_params=pltpu.CompilerParams(vmem_limit_bytes=56 * 1024 * 1024),
         name="level_sums",
     )(own, coefs, mean, far_mean, traits, *others)
 
 
-def swapped(x, bit):
-    return lax.ppermute(x, "samp", [(i, i ^ (1 << bit)) for i in range(lax.axis_size("samp"))])
-
-
-def place_bit(bit):
-    return lax.rem(lax.div(lax.axis_index("samp"), 1 << bit), 2)
+def swapped(x, pair):
+    return lax.ppermute(x, "samp", [(i, i ^ (1 << pair[i % 2])) for i in range(lax.axis_size("samp"))])
+
+
+def place_bit(pair):
+    rank = lax.axis_index("samp")
+    unit = jnp.where(lax.rem(rank, 2) == 0, 1 << pair[0], 1 << pair[1])
+    return lax.rem(lax.div(rank, unit.astype(rank.dtype)), 2)
 
 
 def stack_kernel(near_ref, far_ref, piece_ref, out_ref):
@@ -386,36 +386,33 @@
     )(near, far, piece)
 
 
-def halved(x, bit):
+def halved(x, pair):
     rows = x.shape[0] // 2
-    mine = place_bit(bit)
-    far = swapped(lax.dynamic_slice_in_dim(x, (1 - mine) * rows, rows, 0), bit)
+    mine = place_bit(pair)
+    far = swapped(lax.dynamic_slice_in_dim(x, (1 - mine) * rows, rows, 0), pair)
     return lax.dynamic_slice_in_dim(x, mine * rows, rows, 0) + far
 
 
-def doubled(x, bit):
-    far = swapped(x, bit)
-    even = place_bit(bit) == 0
+def doubled(x, pair):
+    far = swapped(x, pair)
+    even = place_bit(pair) == 0
     return jnp.concatenate([jnp.where(even, x, far), jnp.where(even, far, x)], axis=0)
 
 
 def all_sums(x, away):
     bits = list(range(1, lax.axis_size("samp").bit_length() - 1))
-    x = x + swapped(away, 0)
-    rows = x.shape[0] // 2
-    near = []
-    for part, order in ((x[:rows], bits), (x[rows:], bits[1:] + bits[:1])):
-        for bit in order:
-            part = halved(part, bit)
-        for bit in reversed(order):
-            part = doubled(part, bit)
-        near.append(part)
-    return near + [swapped(part, 0) for part in near]
+    pairs = list(zip(bits, bits[1:] + bits[:1]))
+    x = x + swapped(away, (0, 0))
+    for pair in pairs:
+        x = halved(x, pair)
+    for pair in reversed(pairs):
+        x = doubled(x, pair)
+    return [x, swapped(x, (0, 0))]
 
 
 def small_sum(x):
     for bit in range(lax.axis_size("samp").bit_length() - 1):
-        x = x + swapped(x, bit)
+        x = x + swapped(x, (bit, bit))
     return x
 
 
@@ -445,7 +442,7 @@
     samp_rank = lax.axis_index("samp")
     blk_rank = lax.axis_index("blk")
     paired = nblk == 2
-    place = jnp.stack([blk_rank if paired else jnp.int32(0), place_bit(0)])
+    place = jnp.stack([blk_rank if paired else jnp.int32(0), place_bit((0, 0))])
     turned = traits.T
     near, away, kept, *sent = gram(genotypes, turned, place, members)
     others = [lax.ppermute(piece, "blk", [(0, 1), (1, 0)]) for piece in sent] if paired else []

time: 197 us -> 239 us (1.21)
  waiting for transfers between devices: 74 us -> 114 us
  starting transfers between devices: 29.8 us -> 34.4 us
    ppermute x2, waiting for transfers between devices: 0.01 us -> 36.9 us  [local(): lax.ppermute(piece, 'blk', [(0, 1), (1, 0)])]
    ppermute x19 -> x12, starting transfers between devices: 22.1 us -> 26.6 us  [swapped(): lax.ppermute(x, 'samp', [(i, i ^ 1 << pair[i % 2]) for i in range(lax.axi...]
    all_gather x1, waiting for transfers between devices: 17 us -> 20 us  [local(): coefs = lax.all_gather(both, 'samp', axis_index_groups=groups)]
    ppermute x19 -> x12, waiting for transfers between devices: 48.7 us -> 49 us  [swapped(): lax.ppermute(x, 'samp', [(i, i ^ 1 << pair[i % 2]) for i in range(lax.axi...]
  transfers between devices with their start and end apart: 25 -> 18, of which waited for: 20 -> 16; matrix products, arithmetic and copies ran while one was open for 2% -> 1% of each run, Pallas kernels for 21% -> 17%
where the time goes in v2:
time: 239 us
  waiting for transfers between devices  114 us (48%)
  Pallas kernels  67.6 us (28%)
  starting transfers between devices  34.4 us (14%)
  between operations  14.2 us (6%)
  local copies, waits for them, and re-layouts  5.29 us (2%)
  other arithmetic  3.63 us (2%)
    ppermute x12, waiting for transfers between devices, swapped(): lax.ppermute(x, 'samp', [(i, i ^ 1 << pair[i % 2]) for i in range(lax.axi...  49 us
    pallas_call x1, Pallas kernels, solve(): pl.pallas_call(functools.partial(solve_kernel, nsamp, ntraits), out_shape...  41.1 us
    ppermute x2, waiting for transfers between devices, local(): lax.ppermute(piece, 'blk', [(0, 1), (1, 0)])  36.9 us
    ppermute x12, starting transfers between devices, swapped(): lax.ppermute(x, 'samp', [(i, i ^ 1 << pair[i % 2]) for i in range(lax.axi...  26.6 us
    all_gather x1, waiting for transfers between devices, local(): coefs = lax.all_gather(both, 'samp', axis_index_groups=groups)  20 us
    pallas_call x1, Pallas kernels, gram(): pl.pallas_call(functools.partial(gram_kernel, ntraits), grid_spec=pltpu.P...  14.6 us
    pallas_call x1, Pallas kernels, level_sums(): pl.pallas_call(functools.partial(level_kernel, npen), out_shape=jax.Shape...  10.3 us
  transfers between devices with their start and end apart: 18, of which 16 were waited for; matrix products, arithmetic and copies ran while one was open for 1% of the time, Pallas kernels for 17%

profile of v2, /device:TPU:0, one launch (start us, length us, event | category | flops | bytes accessed | tf_op | source)
XLA Modules:
  0.0 238.7 jit_solution(2805016663435403337)
XLA Ops:
  7.3 1.0 copy-done.1
  8.3 14.6 %gram_sums.1 = (f32[2624,128]{1,0:T(8,128)S(1)}, f32[2624,128]{1,0:T(8,128)S(1)}, bf16[2048,1024]{1,0:T(8,128)(2,1)}, bf16[1024,1024]{1,0:T(8,128)(2,1)}, bf16[1024,1024]{1,0:T(8,128)(2,1)}) custom-call(s32[2]{0:T(128)S(1)} %pad_add_fusion.rank_ref, s32[4096,1024]{1,0:T(8,128)} %geno_ref.1, bf16[64,4096]{1,0:T(8,128)(2,1)S(1)} %bitcast.10), custom_call_target="tpu_custom_call" | custom-call | tf_op jit(solution)/shard_map/gram_sums/pallas_call | solution.py:205
  22.9 0.5 collective-permute-start
  23.3 2.8 %collective-permute-done = f32[2624,128]{1,0:T(8,128)} collective-permute-done((f32[2624,128]{1,0:T(8,128)S(1)}, f32[2624,128]{1,0:T(8,128)}, u32[]{:S(2)}, u32[]{:S(2)}) %collective-permute-start) | collective-permute-done | bytes 1343520 | tf_op jit(solution)/shard_map/ppermute | solution.py:363
  26.2 1.5 add.66
  27.7 2.9 %collective-permute-start.1 = (f32[1312,128]{1,0:T(8,128)S(1)}, f32[1312,128]{1,0:T(8,128)S(1)}, u32[]{:S(2)}, u32[]{:S(2)}) collective-permute-start(f32[1312,128]{1,0:T(8,128)S(1)} %constant_dynamic-slice_fusion.2), channel_id=1, source_target_pairs={{0,4},{2,10},{4,0},{6,14},{8,12},{10,2},{12,8},{14,6},{16,20},{18,... | collective-permute-start | bytes 2015240 | tf_op jit(solution)/shard_map/ppermute | solution.py:363
  30.7 8.7 %collective-permute-done.1 = f32[1312,128]{1,0:T(8,128)S(1)} collective-permute-done((f32[1312,128]{1,0:T(8,128)S(1)}, f32[1312,128]{1,0:T(8,128)S(1)}, u32[]{:S(2)}, u32[]{:S(2)}) %collective-permute-start.1) | collective-permute-done | bytes 671776 | tf_op jit(solution)/shard_map/ppermute | solution.py:363
  39.5 2.1 collective-permute-start.2
  41.7 7.6 %collective-permute-done.2 = f32[656,128]{1,0:T(8,128)S(1)} collective-permute-done((f32[656,128]{1,0:T(8,128)S(1)}, f32[656,128]{1,0:T(8,128)S(1)}, u32[]{:S(2)}, u32[]{:S(2)}) %collective-permute-start.2) | collective-permute-done | bytes 335904 | tf_op jit(solution)/shard_map/ppermute | solution.py:363
  49.4 3.2 %collective-permute-start.3 = (f32[328,128]{1,0:T(8,128)S(1)}, f32[328,128]{1,0:T(8,128)S(1)}, u32[]{:S(2)}, u32[]{:S(2)}) collective-permute-start(f32[328,128]{1,0:T(8,128)S(1)} %constant_dynamic-slice_fusion), channel_id=1, source_target_pairs={{0,16},{2,6},{4,20},{6,2},{8,24},{10,14},{12,28},{14,10},{16,0},{1... | collective-permute-start | bytes 503816 | tf_op jit(solution)/shard_map/ppermute | solution.py:363
  52.5 3.3 %collective-permute-done.3 = f32[328,128]{1,0:T(8,128)S(1)} collective-permute-done((f32[328,128]{1,0:T(8,128)S(1)}, f32[328,128]{1,0:T(8,128)S(1)}, u32[]{:S(2)}, u32[]{:S(2)}) %collective-permute-start.3) | collective-permute-done | bytes 167968 | tf_op jit(solution)/shard_map/ppermute | solution.py:363
  55.9 3.1 %collective-permute-start.4 = (f32[328,128]{1,0:T(8,128)S(1)}, f32[328,128]{1,0:T(8,128)S(1)}, u32[]{:S(2)}, u32[]{:S(2)}) collective-permute-start(f32[328,128]{1,0:T(8,128)S(1)} %dynamic-slice_add_fusion.2), channel_id=1, source_target_pairs={{0,16},{2,6},{4,20},{6,2},{8,24},{10,14},{12,28},{14,10},{16,0},{1... | collective-permute-start | bytes 503816 | tf_op jit(solution)/shard_map/ppermute | solution.py:363
  59.0 4.0 %collective-permute-done.4 = f32[328,128]{1,0:T(8,128)S(1)} collective-permute-done((f32[328,128]{1,0:T(8,128)S(1)}, f32[328,128]{1,0:T(8,128)S(1)}, u32[]{:S(2)}, u32[]{:S(2)}) %collective-permute-start.4) | collective-permute-done | bytes 167968 | tf_op jit(solution)/shard_map/ppermute | solution.py:363
  63.0 7.6 %collective-permute-start.5 = (f32[656,128]{1,0:T(8,128)S(1)}, f32[656,128]{1,0:T(8,128)S(1)}, u32[]{:S(2)}, u32[]{:S(2)}) collective-permute-start(f32[656,128]{1,0:T(8,128)S(1)} %pad_maximum_fusion.2), channel_id=1, source_target_pairs={{0,8},{2,18},{4,12},{6,22},{8,0},{10,26},{12,4},{14,30},{16,24},{1... | collective-permute-start | bytes 1007624 | tf_op jit(solution)/shard_map/ppermute | solution.py:363
  70.6 6.3 %collective-permute-done.5 = f32[656,128]{1,0:T(8,128)S(1)} collective-permute-done((f32[656,128]{1,0:T(8,128)S(1)}, f32[656,128]{1,0:T(8,128)S(1)}, u32[]{:S(2)}, u32[]{:S(2)}) %collective-permute-start.5) | collective-permute-done | bytes 335904 | tf_op jit(solution)/shard_map/ppermute | solution.py:363
  77.0 0.9 pad_maximum_fusion.1
  77.9 1.5 collective-permute-start.6
  79.4 1.5 collective-permute-start.8
  80.9 8.0 %collective-permute-done.6 = f32[1312,128]{1,0:T(8,128)S(1)} collective-permute-done((f32[1312,128]{1,0:T(8,128)}, f32[1312,128]{1,0:T(8,128)S(1)}, u32[]{:S(2)}, u32[]{:S(2)}) %collective-permute-start.6) | collective-permute-done | bytes 671776 | tf_op jit(solution)/shard_map/ppermute | solution.py:363
  88.8 0.1 broadcast_select_fusion.1
  88.9 0.1 pad_maximum_fusion.near
  89.1 1.6 collective-permute-start.10
  90.7 0.6 dynamic_slice.28
  91.3 36.9 %collective-permute-done.8.refs_0_ = bf16[1024,1024]{1,0:T(8,128)(2,1)S(1)} collective-permute-done((bf16[1024,1024]{1,0:T(8,128)(2,1)}, bf16[1024,1024]{1,0:T(8,128)(2,1)S(1)}, u32[]{:S(2)}, u32[]{:S(2)}) %collective-permute-start.8) | collective-permute-done | bytes 2097184 | tf_op jit(solution)/shard_map/ppermute | solution.py:448
  128.2 41.1 %ridge_solve.1 = (bf16[64,1024]{1,0:T(8,128)(2,1)S(1)}, f32[8,1024]{1,0:T(8,128)S(1)}) custom-call(f32[1,1]{1,0:T(1,128)} %bitcast.3.lam_ref, f32[2624,128]{1,0:T(8,128)S(1)} %pad_maximum_fusion.near, f32[2624,128]{1,0:T(8,128)} %collective-permute-done.7.far, bf16[1024,1024]{1,0:T(8,128)(2,1)S(1)} %collective-permute-done.8.refs_0_), custom_call_target="tpu_custom_call" | custom-call | flops 46000001024 | bytes 1000000 | tf_op jit(solution)/shard_map/ridge_solve/pallas_call | solution.py:292
  169.3 0.6 copy-done.3
  169.9 1.5 collective-permute-start.9
  171.4 3.5 %collective-permute-done.9.far_ref = bf16[64,1024]{1,0:T(8,128)(2,1)S(1)} collective-permute-done((bf16[64,1024]{1,0:T(8,128)(2,1)S(1)}, bf16[64,1024]{1,0:T(8,128)(2,1)S(1)}, u32[]{:S(2)}, u32[]{:S(2)}) %collective-permute-start.9) | collective-permute-done | bytes 131104 | tf_op jit(solution)/shard_map/ppermute | solution.py:458
  174.9 0.7 copy-done.5
  175.6 1.7 stack_blocks.1
  177.3 1.6 collective-permute-start.11
  178.9 0.7 dynamic-slice_bitcast_fusion.traits_ref
  179.6 1.7 collective-permute-done.11.far_mean_ref
  181.3 20.0 %all-gather.3.cloned.1.call-done = bf16[16,64,1024]{2,1,0:T(8,128)(2,1)} async-done(((bf16[2,64,1024]{2,1,0:T(8,128)(2,1)}), bf16[16,64,1024]{2,1,0:T(8,128)(2,1)}) %all-gather.3.cloned.1.call-update) | async-done | bytes 2097168 | tf_op jit(solution)/shard_map/all_gather | solution.py:461
  201.3 10.3 %level_sums.1 = f32[64,128]{1,0:T(8,128)} custom-call(bf16[2048,1024]{1,0:T(8,128)(2,1)} %get-tuple-element.9.own_ref, bf16[8,2,64,1024]{3,2,1,0:T(8,128)(2,1)} %bitcast.11, f32[8,1024]{1,0:T(8,128)} %copy-done.4, f32[8,1024]{1,0:T(8,128)} %copy-done.6, bf16[64,2048]{1,0:T(8,128)(2,1)} %dynamic-slice_bitcast_fusion.traits_ref, bf16[1024,1024]{1,0:T(8,128)(2,1)} %copy-done, ...), custom_call_target="tpu_custom_call" | custom-call | tf_op jit(solution)/shard_map/level_sums/pallas_call | solution.py:349
  211.6 1.6 collective-permute-start.12
  213.2 2.5 %collective-permute-done.12 = f32[64,128]{1,0:T(8,128)S(1)} collective-permute-done((f32[64,128]{1,0:T(8,128)}, f32[64,128]{1,0:T(8,128)S(1)}, u32[]{:S(2)}, u32[]{:S(2)}) %collective-permute-start.12) | collective-permute-done | bytes 32800 | tf_op jit(solution)/shard_map/ppermute | solution.py:466
  215.7 0.8 add.77
  216.4 1.2 collective-permute-done.13
  217.7 1.5 collective-permute-start.14
  219.2 2.4 %collective-permute-done.14 = f32[64,128]{1,0:T(8,128)S(1)} collective-permute-done((f32[64,128]{1,0:T(8,128)S(1)}, f32[64,128]{1,0:T(8,128)S(1)}, u32[]{:S(2)}, u32[]{:S(2)}) %collective-permute-start.14) | collective-permute-done | bytes 32800 | tf_op jit(solution)/shard_map/ppermute | solution.py:363
  221.6 1.6 collective-permute-start.15
  223.2 2.3 collective-permute-done.15
  225.5 2.6 %collective-permute-start.16 = (f32[64,128]{1,0:T(8,128)S(1)}, f32[64,128]{1,0:T(8,128)S(1)}, u32[]{:S(2)}, u32[]{:S(2)}) collective-permute-start(f32[64,128]{1,0:T(8,128)S(1)} %add.80), channel_id=1, source_target_pairs={{0,16},{2,18},{4,20},{6,22},{8,24},{10,26},{12,28},{14,30},{16,0},... | collective-permute-start | bytes 98312 | tf_op jit(solution)/shard_map/ppermute | solution.py:363
  228.1 2.2 collective-permute-done.16
  230.4 0.1 copy.9
  230.5 0.6 reshape.11
  231.1 0.7 copy.10
  (35 shorter events, 0.7 us)
Async XLA Ops:
  7.2 194.1 %all-gather.3.cloned.1.call-start = ((), (), s32[]{:S(2)}) async-start(), calls=%async_computation | async-start | bytes 2359296 | tf_op jit(solution)/shard_map/all_gather | solution.py:461
  7.3 1.0 copy-start.1
  22.9 3.3 %collective-permute-start = (f32[2624,128]{1,0:T(8,128)S(1)}, f32[2624,128]{1,0:T(8,128)}, u32[]{:S(2)}, u32[]{:S(2)}) collective-permute-start(f32[2624,128]{1,0:T(8,128)S(1)} %get-tuple-element.11), channel_id=1, source_target_pairs={{0,2},{2,0},{4,6},{6,4},{8,10},{10,8},{12,14},{14,12},{16,18},{18,... | collective-permute-start | bytes 4030472 | tf_op jit(solution)/shard_map/ppermute | solution.py:363
  27.7 11.7 %collective-permute-start.1 = (f32[1312,128]{1,0:T(8,128)S(1)}, f32[1312,128]{1,0:T(8,128)S(1)}, u32[]{:S(2)}, u32[]{:S(2)}) collective-permute-start(f32[1312,128]{1,0:T(8,128)S(1)} %constant_dynamic-slice_fusion.2), channel_id=1, source_target_pairs={{0,4},{2,10},{4,0},{6,14},{8,12},{10,2},{12,8},{14,6},{16,20},{18,... | collective-permute-start | bytes 2015240 | tf_op jit(solution)/shard_map/ppermute | solution.py:363
  39.5 9.8 %collective-permute-start.2 = (f32[656,128]{1,0:T(8,128)S(1)}, f32[656,128]{1,0:T(8,128)S(1)}, u32[]{:S(2)}, u32[]{:S(2)}) collective-permute-start(f32[656,128]{1,0:T(8,128)S(1)} %constant_dynamic-slice_fusion.1), channel_id=1, source_target_pairs={{0,8},{2,18},{4,12},{6,22},{8,0},{10,26},{12,4},{14,30},{16,24},{1... | collective-permute-start | bytes 1007624 | tf_op jit(solution)/shard_map/ppermute | solution.py:363
  49.4 6.5 %collective-permute-start.3 = (f32[328,128]{1,0:T(8,128)S(1)}, f32[328,128]{1,0:T(8,128)S(1)}, u32[]{:S(2)}, u32[]{:S(2)}) collective-permute-start(f32[328,128]{1,0:T(8,128)S(1)} %constant_dynamic-slice_fusion), channel_id=1, source_target_pairs={{0,16},{2,6},{4,20},{6,2},{8,24},{10,14},{12,28},{14,10},{16,0},{1... | collective-permute-start | bytes 503816 | tf_op jit(solution)/shard_map/ppermute | solution.py:363
  55.9 7.1 %collective-permute-start.4 = (f32[328,128]{1,0:T(8,128)S(1)}, f32[328,128]{1,0:T(8,128)S(1)}, u32[]{:S(2)}, u32[]{:S(2)}) collective-permute-start(f32[328,128]{1,0:T(8,128)S(1)} %dynamic-slice_add_fusion.2), channel_id=1, source_target_pairs={{0,16},{2,6},{4,20},{6,2},{8,24},{10,14},{12,28},{14,10},{16,0},{1... | collective-permute-start | bytes 503816 | tf_op jit(solution)/shard_map/ppermute | solution.py:363
  63.0 13.9 %collective-permute-start.5 = (f32[656,128]{1,0:T(8,128)S(1)}, f32[656,128]{1,0:T(8,128)S(1)}, u32[]{:S(2)}, u32[]{:S(2)}) collective-permute-start(f32[656,128]{1,0:T(8,128)S(1)} %pad_maximum_fusion.2), channel_id=1, source_target_pairs={{0,8},{2,18},{4,12},{6,22},{8,0},{10,26},{12,4},{14,30},{16,24},{1... | collective-permute-start | bytes 1007624 | tf_op jit(solution)/shard_map/ppermute | solution.py:363
  77.9 11.0 %collective-permute-start.6 = (f32[1312,128]{1,0:T(8,128)}, f32[1312,128]{1,0:T(8,128)S(1)}, u32[]{:S(2)}, u32[]{:S(2)}) collective-permute-start(f32[1312,128]{1,0:T(8,128)} %pad_maximum_fusion.1), channel_id=1, source_target_pairs={{0,4},{2,10},{4,0},{6,14},{8,12},{10,2},{12,8},{14,6},{16,20},{18,... | collective-permute-start | bytes 2015240 | tf_op jit(solution)/shard_map/ppermute | solution.py:363
  79.4 48.8 %collective-permute-start.8 = (bf16[1024,1024]{1,0:T(8,128)(2,1)}, bf16[1024,1024]{1,0:T(8,128)(2,1)S(1)}, u32[]{:S(2)}, u32[]{:S(2)}) collective-permute-start(bf16[1024,1024]{1,0:T(8,128)(2,1)} %get-tuple-element.12), channel_id=1, source_target_pairs={{0,1},{1,0},{2,3},{3,2},{4,5},{5,4},{6,7},{7,6},{8,9},{9,8},{10,11... | collective-permute-start | bytes 6291464 | tf_op jit(solution)/shard_map/ppermute | solution.py:448
  88.9 1.7 copy-start.7
  89.0 39.1 %collective-permute-start.7 = (f32[2624,128]{1,0:T(8,128)S(1)}, f32[2624,128]{1,0:T(8,128)}, u32[]{:S(2)}, u32[]{:S(2)}) collective-permute-start(f32[2624,128]{1,0:T(8,128)S(1)} %pad_maximum_fusion.near), channel_id=1, source_target_pairs={{0,2},{2,0},{4,6},{6,4},{8,10},{10,8},{12,14},{14,12},{16,18},{18,... | collective-permute-start | bytes 4030472 | tf_op jit(solution)/shard_map/ppermute | solution.py:363
  89.1 82.3 %collective-permute-start.10 = (bf16[1024,1024]{1,0:T(8,128)(2,1)}, bf16[1024,1024]{1,0:T(8,128)(2,1)}, u32[]{:S(2)}, u32[]{:S(2)}) collective-permute-start(bf16[1024,1024]{1,0:T(8,128)(2,1)} %get-tuple-element.14), channel_id=1, source_target_pairs={{0,1},{1,0},{2,3},{3,2},{4,5},{5,4},{6,7},{7,6},{8,9},{9,8},{10,11... | collective-permute-start | bytes 6291464 | tf_op jit(solution)/shard_map/ppermute | solution.py:448
  128.2 41.1 %copy-start = (bf16[1024,1024]{1,0:T(8,128)(2,1)}, bf16[1024,1024]{1,0:T(8,128)(2,1)S(1)}, u32[]{:S(2)}) copy-start(bf16[1024,1024]{1,0:T(8,128)(2,1)S(1)} %collective-permute-done.8.refs_0_) | copy-start | bytes 6291460
  169.3 0.7 copy-start.3
  169.3 8.0 %copy-start.4 = (f32[8,1024]{1,0:T(8,128)}, f32[8,1024]{1,0:T(8,128)S(1)}, u32[]{:S(2)}) copy-start(f32[8,1024]{1,0:T(8,128)S(1)} %get-tuple-element.15.mean_ref) | copy-start | bytes 98308
  169.9 8.9 %copy-start.2 = (bf16[4096,64]{0,1:T(8,128)(2,1)S(1)}, bf16[4096,64]{0,1:T(8,128)(2,1)}, u32[]{:S(2)}) copy-start(bf16[4096,64]{0,1:T(8,128)(2,1)} %param.4) | copy-start | bytes 1572868
  169.9 5.0 %collective-permute-start.9 = (bf16[64,1024]{1,0:T(8,128)(2,1)S(1)}, bf16[64,1024]{1,0:T(8,128)(2,1)S(1)}, u32[]{:S(2)}, u32[]{:S(2)}) collective-permute-start(bf16[64,1024]{1,0:T(8,128)(2,1)S(1)} %get-tuple-element.13.near_ref), channel_id=1, source_target_pairs={{0,1},{1,0},{2,3},{3,2},{4,5},{5,4},{6,7},{7,6},{8,9},{9,8},{10,11... | collective-permute-start | bytes 393224 | tf_op jit(solution)/shard_map/ppermute | solution.py:458
  174.9 0.7 copy-start.5
  177.3 4.0 %collective-permute-start.11 = (f32[8,1024]{1,0:T(8,128)S(1)}, f32[8,1024]{1,0:T(8,128)S(1)}, u32[]{:S(2)}, u32[]{:S(2)}) collective-permute-start(f32[8,1024]{1,0:T(8,128)S(1)} %get-tuple-element.15.mean_ref), channel_id=1, source_target_pairs={{0,1},{1,0},{2,3},{3,2},{4,5},{5,4},{6,7},{7,6},{8,9},{9,8},{10,11... | collective-permute-start | bytes 98312 | tf_op jit(solution)/shard_map/ppermute | solution.py:459
  181.3 20.0 %copy-start.6 = (f32[8,1024]{1,0:T(8,128)}, f32[8,1024]{1,0:T(8,128)S(1)}, u32[]{:S(2)}) copy-start(f32[8,1024]{1,0:T(8,128)S(1)} %collective-permute-done.11.far_mean_ref) | copy-start | bytes 98308
  211.6 4.1 %collective-permute-start.12 = (f32[64,128]{1,0:T(8,128)}, f32[64,128]{1,0:T(8,128)S(1)}, u32[]{:S(2)}, u32[]{:S(2)}) collective-permute-start(f32[64,128]{1,0:T(8,128)} %level_sums.1), channel_id=1, source_target_pairs={{0,1},{1,0},{2,3},{3,2},{4,5},{5,4},{6,7},{7,6},{8,9},{9,8},{10,11... | collective-permute-start | bytes 98312 | tf_op jit(solution)/shard_map/ppermute | solution.py:466
  216.4 1.2 collective-permute-start.13
  217.7 3.9 %collective-permute-start.14 = (f32[64,128]{1,0:T(8,128)S(1)}, f32[64,128]{1,0:T(8,128)S(1)}, u32[]{:S(2)}, u32[]{:S(2)}) collective-permute-start(f32[64,128]{1,0:T(8,128)S(1)} %add.78), channel_id=1, source_target_pairs={{0,4},{2,6},{4,0},{6,2},{8,12},{10,14},{12,8},{14,10},{16,20},{18,... | collective-permute-start | bytes 98312 | tf_op jit(solution)/shard_map/ppermute | solution.py:363
  221.6 3.9 %collective-permute-start.15 = (f32[64,128]{1,0:T(8,128)S(1)}, f32[64,128]{1,0:T(8,128)S(1)}, u32[]{:S(2)}, u32[]{:S(2)}) collective-permute-start(f32[64,128]{1,0:T(8,128)S(1)} %add.79), channel_id=1, source_target_pairs={{0,8},{2,10},{4,12},{6,14},{8,0},{10,2},{12,4},{14,6},{16,24},{18,... | collective-permute-start | bytes 98312 | tf_op jit(solution)/shard_map/ppermute | solution.py:363
  225.5 4.8 %collective-permute-start.16 = (f32[64,128]{1,0:T(8,128)S(1)}, f32[64,128]{1,0:T(8,128)S(1)}, u32[]{:S(2)}, u32[]{:S(2)}) collective-permute-start(f32[64,128]{1,0:T(8,128)S(1)} %add.80), channel_id=1, source_target_pairs={{0,16},{2,18},{4,20},{6,22},{8,24},{10,26},{12,28},{14,30},{16,0},... | collective-permute-start | bytes 98312 | tf_op jit(solution)/shard_map/ppermute | solution.py:363
Sparse Core Ops, SparseCore 0:
  177.4 23.8 all-gather.2

commit v3 on v1

--- a/solution.py
+++ b/solution.py
@@ -279,13 +279,14 @@
             if j == k + 1:
                 inverse = invert_tile(aug[top:top + BLK, top:top + BLK])
             j += size // BLK
-    solved = wide[nvars:end, nvars - BLK:nvars]
-    coef_ref[:, nvars - BLK:nvars] = solved.astype(jnp.bfloat16)
-    for k in range(nblocks - 2, -1, -1):
-        span = slice(BLK * k, BLK * (k + 1))
-        found = wide[nvars:end, span] - dot_hi(solved, wide[BLK * (k + 1):nvars, span])
-        coef_ref[:, span] = found.astype(jnp.bfloat16)
-        solved = jnp.concatenate([found, solved], axis=1)
+    left_over = wide[nvars:end, :]
+    for k in range(nblocks - 1, -1, -1):
+        low_k = BLK * k
+        found = left_over[:, low_k:]
+        coef_ref[:, low_k:low_k + BLK] = found.astype(jnp.bfloat16)
+        if k > 0:
+            rows = as_right(wide[low_k:low_k + BLK, 0:low_k], 0)
+            left_over = left_over[:, 0:low_k] - jnp.dot(as_left(found), rows, preferred_element_type=jnp.float32)
 
 
 def solve(pieces, lam, arrived, nsamp, nvars, ntraits):

time: 197 us -> 196 us (level)
  transfers between devices with their start and end apart: 25 -> 25, of which waited for: 20 -> 21; matrix products, arithmetic and copies ran while one was open for 2% -> 2% of each run, Pallas kernels for 21% -> 21%
where the time goes in v3:
time: 196 us
  waiting for transfers between devices  74 us (38%)
  Pallas kernels  67.5 us (34%)
  starting transfers between devices  29.8 us (15%)
  between operations  14.3 us (7%)
  local copies, waits for them, and re-layouts  5.54 us (3%)
  other arithmetic  4.68 us (2%)
    ppermute x19, waiting for transfers between devices, swapped(): lax.ppermute(x, 'samp', [(i, i ^ 1 << bit) for i in range(lax.axis_size('...  48.7 us
    pallas_call x1, Pallas kernels, solve(): pl.pallas_call(functools.partial(solve_kernel, nsamp, ntraits), out_shape...  40.9 us
    ppermute x19, starting transfers between devices, swapped(): lax.ppermute(x, 'samp', [(i, i ^ 1 << bit) for i in range(lax.axis_size('...  22.1 us
    all_gather x1, waiting for transfers between devices, local(): coefs = lax.all_gather(both, 'samp', axis_index_groups=groups)  17 us
    pallas_call x1, Pallas kernels, gram(): pl.pallas_call(functools.partial(gram_kernel, ntraits), grid_spec=pltpu.P...  14.7 us
    pallas_call x1, Pallas kernels, level_sums(): pl.pallas_call(functools.partial(level_kernel, npen), out_shape=jax.Shape...  10.3 us
  transfers between devices with their start and end apart: 25, of which 21 were waited for; matrix products, arithmetic and copies ran while one was open for 2% of the time, Pallas kernels for 21%

profile of v3, /device:TPU:0, one launch (start us, length us, event | category | flops | bytes accessed | tf_op | source)
XLA Modules:
  0.0 195.9 jit_solution(16175529656727614032)
XLA Ops:
  7.3 1.0 copy-done.1
  8.3 14.7 %gram_sums.1 = (f32[2688,128]{1,0:T(8,128)S(1)}, f32[2688,128]{1,0:T(8,128)S(1)}, bf16[2048,1024]{1,0:T(8,128)(2,1)}, bf16[1088,1024]{1,0:T(8,128)(2,1)}, bf16[960,1024]{1,0:T(8,128)(2,1)}) custom-call(s32[2]{0:T(128)S(1)} %pad_add_fusion.rank_ref, s32[4096,1024]{1,0:T(8,128)} %geno_ref.1, bf16[64,4096]{1,0:T(8,128)(2,1)S(1)} %bitcast.10), custom_call_target="tpu_custom_call" | custom-call | tf_op jit(solution)/shard_map/gram_sums/pallas_call | solution.py:205
  23.4 2.9 %collective-permute-done = f32[2688,128]{1,0:T(8,128)} collective-permute-done((f32[2688,128]{1,0:T(8,128)S(1)}, f32[2688,128]{1,0:T(8,128)}, u32[]{:S(2)}, u32[]{:S(2)}) %collective-permute-start) | collective-permute-done | bytes 1376288 | tf_op jit(solution)/shard_map/ppermute | solution.py:366
  26.3 1.5 add.93
  27.9 0.8 constant_dynamic-slice_fusion.2
  28.7 3.0 %collective-permute-start.7 = (f32[672,128]{1,0:T(8,128)}, f32[672,128]{1,0:T(8,128)S(1)}, u32[]{:S(2)}, u32[]{:S(2)}) collective-permute-start(f32[672,128]{1,0:T(8,128)} %constant_dynamic-slice_fusion.2), channel_id=1, source_target_pairs={{0,8},{2,10},{4,12},{6,14},{8,0},{10,2},{12,4},{14,6},{16,24},{18,... | collective-permute-start | bytes 1032200 | tf_op jit(solution)/shard_map/ppermute | solution.py:366
  31.7 1.5 collective-permute-start.15
  33.2 1.6 collective-permute-start.1
  34.8 5.5 %collective-permute-done.7 = f32[672,128]{1,0:T(8,128)S(1)} collective-permute-done((f32[672,128]{1,0:T(8,128)}, f32[672,128]{1,0:T(8,128)S(1)}, u32[]{:S(2)}, u32[]{:S(2)}) %collective-permute-start.7) | collective-permute-done | bytes 344096 | tf_op jit(solution)/shard_map/ppermute | solution.py:366
  40.3 1.0 dynamic-slice_add_fusion
  41.3 2.8 %collective-permute-start.8 = (f32[336,128]{1,0:T(8,128)S(1)}, f32[336,128]{1,0:T(8,128)S(1)}, u32[]{:S(2)}, u32[]{:S(2)}) collective-permute-start(f32[336,128]{1,0:T(8,128)S(1)} %constant_dynamic-slice_fusion.1), channel_id=1, source_target_pairs={{0,16},{2,18},{4,20},{6,22},{8,24},{10,26},{12,28},{14,30},{16,0},... | collective-permute-start | bytes 516104 | tf_op jit(solution)/shard_map/ppermute | solution.py:366
  44.2 1.6 collective-permute-start.2
  45.8 6.1 %collective-permute-done.8 = f32[336,128]{1,0:T(8,128)S(1)} collective-permute-done((f32[336,128]{1,0:T(8,128)S(1)}, f32[336,128]{1,0:T(8,128)S(1)}, u32[]{:S(2)}, u32[]{:S(2)}) %collective-permute-start.8) | collective-permute-done | bytes 172064 | tf_op jit(solution)/shard_map/ppermute | solution.py:366
  52.0 1.4 collective-permute-start.9
  53.5 0.6 collective-permute-start.3
  54.1 2.4 %collective-permute-done.9 = f32[168,128]{1,0:T(8,128)S(1)} collective-permute-done((f32[168,128]{1,0:T(8,128)S(1)}, f32[168,128]{1,0:T(8,128)S(1)}, u32[]{:S(2)}, u32[]{:S(2)}) %collective-permute-start.9) | collective-permute-done | bytes 86048 | tf_op jit(solution)/shard_map/ppermute | solution.py:366
  56.6 1.4 collective-permute-start.10
  58.0 2.9 %collective-permute-done.3 = f32[168,128]{1,0:T(8,128)S(1)} collective-permute-done((f32[168,128]{1,0:T(8,128)S(1)}, f32[168,128]{1,0:T(8,128)S(1)}, u32[]{:S(2)}, u32[]{:S(2)}) %collective-permute-start.3) | collective-permute-done | bytes 86048 | tf_op jit(solution)/shard_map/ppermute | solution.py:366
  61.2 2.9 %collective-permute-start.11 = (f32[336,128]{1,0:T(8,128)S(1)}, f32[336,128]{1,0:T(8,128)S(1)}, u32[]{:S(2)}, u32[]{:S(2)}) collective-permute-start(f32[336,128]{1,0:T(8,128)S(1)} %pad_maximum_fusion.5), channel_id=1, source_target_pairs={{0,16},{2,18},{4,20},{6,22},{8,24},{10,26},{12,28},{14,30},{16,0},... | collective-permute-start | bytes 516104 | tf_op jit(solution)/shard_map/ppermute | solution.py:366
  64.1 6.3 %collective-permute-done.4 = f32[168,128]{1,0:T(8,128)S(1)} collective-permute-done((f32[168,128]{1,0:T(8,128)S(1)}, f32[168,128]{1,0:T(8,128)S(1)}, u32[]{:S(2)}, u32[]{:S(2)}) %collective-permute-start.4) | collective-permute-done | bytes 86048 | tf_op jit(solution)/shard_map/ppermute | solution.py:366
  70.4 1.7 collective-permute-done.11
  72.6 5.1 %collective-permute-done.5 = f32[336,128]{1,0:T(8,128)S(1)} collective-permute-done((f32[336,128]{1,0:T(8,128)S(1)}, f32[336,128]{1,0:T(8,128)S(1)}, u32[]{:S(2)}, u32[]{:S(2)}) %collective-permute-start.5) | collective-permute-done | bytes 172064 | tf_op jit(solution)/shard_map/ppermute | solution.py:366
  77.9 3.9 %collective-permute-done.12 = f32[672,128]{1,0:T(8,128)S(1)} collective-permute-done((f32[672,128]{1,0:T(8,128)S(1)}, f32[672,128]{1,0:T(8,128)S(1)}, u32[]{:S(2)}, u32[]{:S(2)}) %collective-permute-start.12) | collective-permute-done | bytes 344096 | tf_op jit(solution)/shard_map/ppermute | solution.py:366
  82.0 3.1 %collective-permute-done.6 = f32[672,128]{1,0:T(8,128)S(1)} collective-permute-done((f32[672,128]{1,0:T(8,128)S(1)}, f32[672,128]{1,0:T(8,128)S(1)}, u32[]{:S(2)}, u32[]{:S(2)}) %collective-permute-start.6) | collective-permute-done | bytes 344096 | tf_op jit(solution)/shard_map/ppermute | solution.py:366
  85.2 0.9 pad_maximum_fusion.near_a
  86.1 1.5 collective-permute-start.17
  88.6 40.9 %ridge_solve.1 = (bf16[64,1024]{1,0:T(8,128)(2,1)S(1)}, f32[8,1024]{1,0:T(8,128)S(1)}) custom-call(f32[1,1]{1,0:T(1,128)} %bitcast.3.lam_ref, f32[1344,128]{1,0:T(8,128)} %pad_maximum_fusion.near_a, f32[1344,128]{1,0:T(8,128)S(1)} %pad_maximum_fusion.1.near_b, f32[1344,128]{1,0:T(8,128)} %collective-permute-done.13.far_a, ...), custom_call_target="tpu_custom_call" | custom-call | flops 46000001024 | bytes 1000000 | tf_op jit(solution)/shard_map/ridge_solve/pallas_call | solution.py:293
  129.5 1.5 collective-permute-start.16
  131.6 3.5 %collective-permute-done.16.far_ref = bf16[64,1024]{1,0:T(8,128)(2,1)S(1)} collective-permute-done((bf16[64,1024]{1,0:T(8,128)(2,1)S(1)}, bf16[64,1024]{1,0:T(8,128)(2,1)S(1)}, u32[]{:S(2)}, u32[]{:S(2)}) %collective-permute-start.16) | collective-permute-done | bytes 131104 | tf_op jit(solution)/shard_map/ppermute | solution.py:462
  135.1 0.6 copy-done.6
  135.8 1.7 stack_blocks.1
  137.5 1.5 collective-permute-start.18
  139.0 0.7 dynamic-slice_bitcast_fusion.traits_ref
  139.8 1.7 collective-permute-done.18.far_mean_ref
  141.5 17.0 %all-gather.3.cloned.1.call-done = bf16[16,64,1024]{2,1,0:T(8,128)(2,1)} async-done(((bf16[2,64,1024]{2,1,0:T(8,128)(2,1)}), bf16[16,64,1024]{2,1,0:T(8,128)(2,1)}) %all-gather.3.cloned.1.call-update) | async-done | bytes 2097168 | tf_op jit(solution)/shard_map/all_gather | solution.py:465
  158.5 10.3 %level_sums.1 = f32[64,128]{1,0:T(8,128)} custom-call(bf16[2048,1024]{1,0:T(8,128)(2,1)} %get-tuple-element.9.own_ref, bf16[8,2,64,1024]{3,2,1,0:T(8,128)(2,1)} %bitcast.11, f32[8,1024]{1,0:T(8,128)} %copy-done.4, f32[8,1024]{1,0:T(8,128)} %copy-done.7, bf16[64,2048]{1,0:T(8,128)(2,1)} %dynamic-slice_bitcast_fusion.traits_ref, bf16[1088,1024]{1,0:T(8,128)(2,1)} %copy-done, ...), custom_call_target="tpu_custom_call" | custom-call | tf_op jit(solution)/shard_map/level_sums/pallas_call | solution.py:351
  168.8 1.6 collective-permute-start.19
  170.4 2.5 %collective-permute-done.19 = f32[64,128]{1,0:T(8,128)S(1)} collective-permute-done((f32[64,128]{1,0:T(8,128)}, f32[64,128]{1,0:T(8,128)S(1)}, u32[]{:S(2)}, u32[]{:S(2)}) %collective-permute-start.19) | collective-permute-done | bytes 32800 | tf_op jit(solution)/shard_map/ppermute | solution.py:470
  172.9 0.8 add.113
  173.7 1.2 collective-permute-done.20
  174.9 1.5 collective-permute-start.21
  176.4 2.4 %collective-permute-done.21 = f32[64,128]{1,0:T(8,128)S(1)} collective-permute-done((f32[64,128]{1,0:T(8,128)S(1)}, f32[64,128]{1,0:T(8,128)S(1)}, u32[]{:S(2)}, u32[]{:S(2)}) %collective-permute-start.21) | collective-permute-done | bytes 32800 | tf_op jit(solution)/shard_map/ppermute | solution.py:366
  178.8 1.6 collective-permute-start.22
  180.4 2.3 %collective-permute-done.22 = f32[64,128]{1,0:T(8,128)S(1)} collective-permute-done((f32[64,128]{1,0:T(8,128)S(1)}, f32[64,128]{1,0:T(8,128)S(1)}, u32[]{:S(2)}, u32[]{:S(2)}) %collective-permute-start.22) | collective-permute-done | bytes 32800 | tf_op jit(solution)/shard_map/ppermute | solution.py:366
  182.7 2.6 %collective-permute-start.23 = (f32[64,128]{1,0:T(8,128)S(1)}, f32[64,128]{1,0:T(8,128)S(1)}, u32[]{:S(2)}, u32[]{:S(2)}) collective-permute-start(f32[64,128]{1,0:T(8,128)S(1)} %add.116), channel_id=1, source_target_pairs={{0,16},{2,18},{4,20},{6,22},{8,24},{10,26},{12,28},{14,30},{16,0},... | collective-permute-start | bytes 98312 | tf_op jit(solution)/shard_map/ppermute | solution.py:366
  185.3 2.2 %collective-permute-done.23 = f32[64,128]{1,0:T(8,128)S(1)} collective-permute-done((f32[64,128]{1,0:T(8,128)S(1)}, f32[64,128]{1,0:T(8,128)S(1)}, u32[]{:S(2)}, u32[]{:S(2)}) %collective-permute-start.23) | collective-permute-done | bytes 32800 | tf_op jit(solution)/shard_map/ppermute | solution.py:366
  187.7 0.6 reshape.11
  188.4 0.7 copy.10
  (64 shorter events, 3.7 us)
Async XLA Ops:
  7.2 151.4 %all-gather.3.cloned.1.call-start = ((), (), s32[]{:S(2)}) async-start(), calls=%async_computation | async-start | bytes 2359296 | tf_op jit(solution)/shard_map/all_gather | solution.py:465
  7.3 1.0 copy-start.1
  23.0 3.3 %collective-permute-start = (f32[2688,128]{1,0:T(8,128)S(1)}, f32[2688,128]{1,0:T(8,128)}, u32[]{:S(2)}, u32[]{:S(2)}) collective-permute-start(f32[2688,128]{1,0:T(8,128)S(1)} %get-tuple-element.11), channel_id=1, source_target_pairs={{0,2},{2,0},{4,6},{6,4},{8,10},{10,8},{12,14},{14,12},{16,18},{18,... | collective-permute-start | bytes 4128776 | tf_op jit(solution)/shard_map/ppermute | solution.py:366
  27.9 3.8 %copy-start.5 = (f32[1344,128]{1,0:T(8,128)}, f32[1344,128]{1,0:T(8,128)S(1)}, u32[]{:S(2)}) copy-start(f32[1344,128]{1,0:T(8,128)S(1)} %get-tuple-element.22) | copy-start | bytes 2064388
  28.7 11.5 %collective-permute-start.7 = (f32[672,128]{1,0:T(8,128)}, f32[672,128]{1,0:T(8,128)S(1)}, u32[]{:S(2)}, u32[]{:S(2)}) collective-permute-start(f32[672,128]{1,0:T(8,128)} %constant_dynamic-slice_fusion.2), channel_id=1, source_target_pairs={{0,8},{2,10},{4,12},{6,14},{8,0},{10,2},{12,4},{14,6},{16,24},{18,... | collective-permute-start | bytes 1032200 | tf_op jit(solution)/shard_map/ppermute | solution.py:366
  31.7 56.5 %collective-permute-start.15 = (bf16[1088,1024]{1,0:T(8,128)(2,1)}, bf16[1088,1024]{1,0:T(8,128)(2,1)S(1)}, u32[]{:S(2)}, u32[]{:S(2)}) collective-permute-start(bf16[1088,1024]{1,0:T(8,128)(2,1)} %get-tuple-element.12), channel_id=1, source_target_pairs={{0,1},{1,0},{2,3},{3,2},{4,5},{5,4},{6,7},{7,6},{8,9},{9,8},{10,11... | collective-permute-start | bytes 6684680 | tf_op jit(solution)/shard_map/ppermute | solution.py:452
  33.2 10.9 %collective-permute-start.1 = (f32[672,128]{1,0:T(8,128)S(1)}, f32[672,128]{1,0:T(8,128)S(1)}, u32[]{:S(2)}, u32[]{:S(2)}) collective-permute-start(f32[672,128]{1,0:T(8,128)S(1)} %constant_dynamic-slice_fusion.5), channel_id=1, source_target_pairs={{0,4},{2,6},{4,0},{6,2},{8,12},{10,14},{12,8},{14,10},{16,20},{18,... | collective-permute-start | bytes 1032200 | tf_op jit(solution)/shard_map/ppermute | solution.py:366
  41.3 10.7 %collective-permute-start.8 = (f32[336,128]{1,0:T(8,128)S(1)}, f32[336,128]{1,0:T(8,128)S(1)}, u32[]{:S(2)}, u32[]{:S(2)}) collective-permute-start(f32[336,128]{1,0:T(8,128)S(1)} %constant_dynamic-slice_fusion.1), channel_id=1, source_target_pairs={{0,16},{2,18},{4,20},{6,22},{8,24},{10,26},{12,28},{14,30},{16,0},... | collective-permute-start | bytes 516104 | tf_op jit(solution)/shard_map/ppermute | solution.py:366
  44.2 9.2 %collective-permute-start.2 = (f32[336,128]{1,0:T(8,128)S(1)}, f32[336,128]{1,0:T(8,128)S(1)}, u32[]{:S(2)}, u32[]{:S(2)}) collective-permute-start(f32[336,128]{1,0:T(8,128)S(1)} %constant_dynamic-slice_fusion.4), channel_id=1, source_target_pairs={{0,8},{2,10},{4,12},{6,14},{8,0},{10,2},{12,4},{14,6},{16,24},{18,... | collective-permute-start | bytes 516104 | tf_op jit(solution)/shard_map/ppermute | solution.py:366
  52.0 4.6 %collective-permute-start.9 = (f32[168,128]{1,0:T(8,128)S(1)}, f32[168,128]{1,0:T(8,128)S(1)}, u32[]{:S(2)}, u32[]{:S(2)}) collective-permute-start(f32[168,128]{1,0:T(8,128)S(1)} %constant_dynamic-slice_fusion), channel_id=1, source_target_pairs={{0,4},{2,6},{4,0},{6,2},{8,12},{10,14},{12,8},{14,10},{16,20},{18,... | collective-permute-start | bytes 258056 | tf_op jit(solution)/shard_map/ppermute | solution.py:366
  53.5 7.5 %collective-permute-start.3 = (f32[168,128]{1,0:T(8,128)S(1)}, f32[168,128]{1,0:T(8,128)S(1)}, u32[]{:S(2)}, u32[]{:S(2)}) collective-permute-start(f32[168,128]{1,0:T(8,128)S(1)} %constant_dynamic-slice_fusion.3), channel_id=1, source_target_pairs={{0,16},{2,18},{4,20},{6,22},{8,24},{10,26},{12,28},{14,30},{16,0},... | collective-permute-start | bytes 258056 | tf_op jit(solution)/shard_map/ppermute | solution.py:366
  56.6 4.6 %collective-permute-start.10 = (f32[168,128]{1,0:T(8,128)S(1)}, f32[168,128]{1,0:T(8,128)S(1)}, u32[]{:S(2)}, u32[]{:S(2)}) collective-permute-start(f32[168,128]{1,0:T(8,128)S(1)} %dynamic-slice_add_fusion.4), channel_id=1, source_target_pairs={{0,4},{2,6},{4,0},{6,2},{8,12},{10,14},{12,8},{14,10},{16,20},{18,... | collective-permute-start | bytes 258056 | tf_op jit(solution)/shard_map/ppermute | solution.py:366
  61.0 9.4 %collective-permute-start.4 = (f32[168,128]{1,0:T(8,128)S(1)}, f32[168,128]{1,0:T(8,128)S(1)}, u32[]{:S(2)}, u32[]{:S(2)}) collective-permute-start(f32[168,128]{1,0:T(8,128)S(1)} %dynamic-slice_add_fusion.5), channel_id=1, source_target_pairs={{0,16},{2,18},{4,20},{6,22},{8,24},{10,26},{12,28},{14,30},{16,0},... | collective-permute-start | bytes 258056 | tf_op jit(solution)/shard_map/ppermute | solution.py:366
  61.2 11.0 %collective-permute-start.11 = (f32[336,128]{1,0:T(8,128)S(1)}, f32[336,128]{1,0:T(8,128)S(1)}, u32[]{:S(2)}, u32[]{:S(2)}) collective-permute-start(f32[336,128]{1,0:T(8,128)S(1)} %pad_maximum_fusion.5), channel_id=1, source_target_pairs={{0,16},{2,18},{4,20},{6,22},{8,24},{10,26},{12,28},{14,30},{16,0},... | collective-permute-start | bytes 516104 | tf_op jit(solution)/shard_map/ppermute | solution.py:366
  70.4 7.4 %collective-permute-start.5 = (f32[336,128]{1,0:T(8,128)S(1)}, f32[336,128]{1,0:T(8,128)S(1)}, u32[]{:S(2)}, u32[]{:S(2)}) collective-permute-start(f32[336,128]{1,0:T(8,128)S(1)} %pad_maximum_fusion.4), channel_id=1, source_target_pairs={{0,8},{2,10},{4,12},{6,14},{8,0},{10,2},{12,4},{14,6},{16,24},{18,... | collective-permute-start | bytes 516104 | tf_op jit(solution)/shard_map/ppermute | solution.py:366
  72.2 9.6 %collective-permute-start.12 = (f32[672,128]{1,0:T(8,128)S(1)}, f32[672,128]{1,0:T(8,128)S(1)}, u32[]{:S(2)}, u32[]{:S(2)}) collective-permute-start(f32[672,128]{1,0:T(8,128)S(1)} %pad_maximum_fusion.3), channel_id=1, source_target_pairs={{0,8},{2,10},{4,12},{6,14},{8,0},{10,2},{12,4},{14,6},{16,24},{18,... | collective-permute-start | bytes 1032200 | tf_op jit(solution)/shard_map/ppermute | solution.py:366
  77.8 7.3 %collective-permute-start.6 = (f32[672,128]{1,0:T(8,128)S(1)}, f32[672,128]{1,0:T(8,128)S(1)}, u32[]{:S(2)}, u32[]{:S(2)}) collective-permute-start(f32[672,128]{1,0:T(8,128)S(1)} %pad_maximum_fusion.2), channel_id=1, source_target_pairs={{0,4},{2,6},{4,0},{6,2},{8,12},{10,14},{12,8},{14,10},{16,20},{18,... | collective-permute-start | bytes 1032200 | tf_op jit(solution)/shard_map/ppermute | solution.py:366
  81.8 5.7 %copy-start.8 = (s32[5]{0:T(128)S(1)}, s32[5]{0:T(128)}, u32[]{:S(2)}) copy-start(s32[5]{0:T(128)} %param.5) | copy-start | bytes 64
  81.9 6.3 %collective-permute-start.14 = (f32[1344,128]{1,0:T(8,128)S(1)}, f32[1344,128]{1,0:T(8,128)}, u32[]{:S(2)}, u32[]{:S(2)}) collective-permute-start(f32[1344,128]{1,0:T(8,128)S(1)} %pad_maximum_fusion.1.near_b), channel_id=1, source_target_pairs={{0,2},{2,0},{4,6},{6,4},{8,10},{10,8},{12,14},{14,12},{16,18},{18,... | collective-permute-start | bytes 2064392 | tf_op jit(solution)/shard_map/ppermute | solution.py:366
  86.1 2.5 %collective-permute-start.13 = (f32[1344,128]{1,0:T(8,128)}, f32[1344,128]{1,0:T(8,128)}, u32[]{:S(2)}, u32[]{:S(2)}) collective-permute-start(f32[1344,128]{1,0:T(8,128)} %pad_maximum_fusion.near_a), channel_id=1, source_target_pairs={{0,2},{2,0},{4,6},{6,4},{8,10},{10,8},{12,14},{14,12},{16,18},{18,... | collective-permute-start | bytes 2064392 | tf_op jit(solution)/shard_map/ppermute | solution.py:366
  86.1 45.5 %collective-permute-start.17 = (bf16[960,1024]{1,0:T(8,128)(2,1)}, bf16[960,1024]{1,0:T(8,128)(2,1)}, u32[]{:S(2)}, u32[]{:S(2)}) collective-permute-start(bf16[960,1024]{1,0:T(8,128)(2,1)} %get-tuple-element.14), channel_id=1, source_target_pairs={{0,1},{1,0},{2,3},{3,2},{4,5},{5,4},{6,7},{7,6},{8,9},{9,8},{10,11... | collective-permute-start | bytes 5898248 | tf_op jit(solution)/shard_map/ppermute | solution.py:452
  88.2 41.3 %copy-start = (bf16[1088,1024]{1,0:T(8,128)(2,1)}, bf16[1088,1024]{1,0:T(8,128)(2,1)S(1)}, u32[]{:S(2)}) copy-start(bf16[1088,1024]{1,0:T(8,128)(2,1)S(1)} %collective-permute-done.15.refs_0_) | copy-start | bytes 6684676
  129.5 5.7 %copy-start.3 = (bf16[64,1024]{1,0:T(8,128)(2,1)}, bf16[64,1024]{1,0:T(8,128)(2,1)S(1)}, u32[]{:S(2)}) copy-start(bf16[64,1024]{1,0:T(8,128)(2,1)S(1)} %get-tuple-element.13.near_ref) | copy-start | bytes 393220
  129.5 29.0 %copy-start.4 = (f32[8,1024]{1,0:T(8,128)}, f32[8,1024]{1,0:T(8,128)S(1)}, u32[]{:S(2)}) copy-start(f32[8,1024]{1,0:T(8,128)S(1)} %get-tuple-element.15.mean_ref) | copy-start | bytes 98308
  129.5 9.5 %copy-start.2 = (bf16[4096,64]{0,1:T(8,128)(2,1)S(1)}, bf16[4096,64]{0,1:T(8,128)(2,1)}, u32[]{:S(2)}) copy-start(bf16[4096,64]{0,1:T(8,128)(2,1)} %param.4) | copy-start | bytes 1572868
  129.5 5.6 %collective-permute-start.16 = (bf16[64,1024]{1,0:T(8,128)(2,1)S(1)}, bf16[64,1024]{1,0:T(8,128)(2,1)S(1)}, u32[]{:S(2)}, u32[]{:S(2)}) collective-permute-start(bf16[64,1024]{1,0:T(8,128)(2,1)S(1)} %get-tuple-element.13.near_ref), channel_id=1, source_target_pairs={{0,1},{1,0},{2,3},{3,2},{4,5},{5,4},{6,7},{7,6},{8,9},{9,8},{10,11... | collective-permute-start | bytes 393224 | tf_op jit(solution)/shard_map/ppermute | solution.py:462
  135.1 0.7 copy-start.6
  137.5 4.0 %collective-permute-start.18 = (f32[8,1024]{1,0:T(8,128)S(1)}, f32[8,1024]{1,0:T(8,128)S(1)}, u32[]{:S(2)}, u32[]{:S(2)}) collective-permute-start(f32[8,1024]{1,0:T(8,128)S(1)} %get-tuple-element.15.mean_ref), channel_id=1, source_target_pairs={{0,1},{1,0},{2,3},{3,2},{4,5},{5,4},{6,7},{7,6},{8,9},{9,8},{10,11... | collective-permute-start | bytes 98312 | tf_op jit(solution)/shard_map/ppermute | solution.py:463
  141.5 17.0 %copy-start.7 = (f32[8,1024]{1,0:T(8,128)}, f32[8,1024]{1,0:T(8,128)S(1)}, u32[]{:S(2)}) copy-start(f32[8,1024]{1,0:T(8,128)S(1)} %collective-permute-done.18.far_mean_ref) | copy-start | bytes 98308
  168.8 4.1 %collective-permute-start.19 = (f32[64,128]{1,0:T(8,128)}, f32[64,128]{1,0:T(8,128)S(1)}, u32[]{:S(2)}, u32[]{:S(2)}) collective-permute-start(f32[64,128]{1,0:T(8,128)} %level_sums.1), channel_id=1, source_target_pairs={{0,1},{1,0},{2,3},{3,2},{4,5},{5,4},{6,7},{7,6},{8,9},{9,8},{10,11... | collective-permute-start | bytes 98312 | tf_op jit(solution)/shard_map/ppermute | solution.py:470
  173.7 1.2 collective-permute-start.20
  174.9 3.9 %collective-permute-start.21 = (f32[64,128]{1,0:T(8,128)S(1)}, f32[64,128]{1,0:T(8,128)S(1)}, u32[]{:S(2)}, u32[]{:S(2)}) collective-permute-start(f32[64,128]{1,0:T(8,128)S(1)} %add.114), channel_id=1, source_target_pairs={{0,4},{2,6},{4,0},{6,2},{8,12},{10,14},{12,8},{14,10},{16,20},{18,... | collective-permute-start | bytes 98312 | tf_op jit(solution)/shard_map/ppermute | solution.py:366
  178.8 3.9 %collective-permute-start.22 = (f32[64,128]{1,0:T(8,128)S(1)}, f32[64,128]{1,0:T(8,128)S(1)}, u32[]{:S(2)}, u32[]{:S(2)}) collective-permute-start(f32[64,128]{1,0:T(8,128)S(1)} %add.115), channel_id=1, source_target_pairs={{0,8},{2,10},{4,12},{6,14},{8,0},{10,2},{12,4},{14,6},{16,24},{18,... | collective-permute-start | bytes 98312 | tf_op jit(solution)/shard_map/ppermute | solution.py:366
  182.7 4.8 %collective-permute-start.23 = (f32[64,128]{1,0:T(8,128)S(1)}, f32[64,128]{1,0:T(8,128)S(1)}, u32[]{:S(2)}, u32[]{:S(2)}) collective-permute-start(f32[64,128]{1,0:T(8,128)S(1)} %add.116), channel_id=1, source_target_pairs={{0,16},{2,18},{4,20},{6,22},{8,24},{10,26},{12,28},{14,30},{16,0},... | collective-permute-start | bytes 98312 | tf_op jit(solution)/shard_map/ppermute | solution.py:366
Sparse Core Ops, SparseCore 0:
  137.6 20.8 all-gather.2
